TPU v7x, 128 devices: a whole 4x4x4 slice. The times are simulated.
128 devices in a mesh: patch: 16 (over y, x_lo, core), head: 8 (over z, x_hi).
Axes of the slice: x: 4 (x_hi: 2, x_lo: 2; x = x_hi * 2 + x_lo), y: 4, z: 4, core: 2. Of those that a mesh axis runs over, the one named last changes fastest.
Arguments:
- image_tokens: bfloat16 [12288, 3072], P('patch', 'head'), may hold values from -1.796875 to 1.796875
- modulation: float32 [2, 3072], replicated, may hold values from -3 to 3
- gate: float32 [3072], P('head'), may hold values from -9 to 9
- w_qkv: bfloat16 [3072, 3, 3072], P(None, None, 'head'), may hold values from -0.109375 to 0.109375
- b_qkv: float32 [3, 3072], P(None, 'head'), may hold values from -1.8 to 1.8
- q_gain: float32 [128], replicated, may hold values from 1 to 2
- k_gain: float32 [128], replicated, may hold values from 1 to 2
- text_gain: float32 [128], replicated, may hold values from 1 to 2
- w_out: bfloat16 [3072, 3072], P('head'), may hold values from -0.15625 to 0.15625
- b_out: float32 [3072], P('head'), may hold values from -1.8 to 1.8
- text_kv: bfloat16 [512, 2, 3072], P(None, None, 'head'), may hold values from -6 to 6
- stale_kv: bfloat16 [12288, 2, 3072], P('patch', None, 'head'), may hold values from -6 to 6
Outputs:
- image_out: bfloat16 [12288, 3072], P('patch', 'head')
- fresh_kv: bfloat16 [12288, 2, 3072], P('patch', None, 'head')
All inputs are finite; a program needn't handle non-finite values.
Results may differ from a plain program's by a relative error of at most 0.015.
Values may be sent and summed in bfloat16 or wider, within the bound.
No kernel may reach another device: no remote copies, remote signals or barrier semaphores. Data moves between devices by JAX's collectives and lax.ppermute only.
A program may use at most 320 MiB of HBM per device.

v0:
```python
import jax
import jax.numpy as jnp
from jax import lax
from jax.sharding import PartitionSpec as P

GRID_W = 256


def angles(positions):
    grid_rows = (positions // GRID_W).astype(jnp.float32)
    grid_cols = (positions % GRID_W).astype(jnp.float32)
    pairs = jnp.arange(64)
    step_row = jnp.clip(pairs - 8, 0, 27).astype(jnp.float32)
    step_col = jnp.clip(pairs - 36, 0, 27).astype(jnp.float32)
    freq_row = jnp.power(10000.0, -2.0 * step_row / 56.0)
    freq_col = jnp.power(10000.0, -2.0 * step_col / 56.0)
    angle = jnp.where(
        pairs[None, :] < 8,
        0.0,
        jnp.where(
            pairs[None, :] < 36,
            grid_rows[:, None] * freq_row[None, :],
            grid_cols[:, None] * freq_col[None, :],
        ),
    )
    angle = jnp.repeat(angle, 2, axis=1)
    return (jnp.cos(angle), jnp.sin(angle))


def head_norm(raw, gain):
    values = raw.astype(jnp.float32)
    return values * lax.rsqrt(jnp.mean(values * values, axis=-1, keepdims=True) + 1e-06) * gain


def rotate(values, positions):
    cosine, sine = angles(positions)
    paired = values.reshape(values.shape[:-1] + (64, 2))
    turned = jnp.stack([-paired[..., 1], paired[..., 0]], axis=-1).reshape(values.shape)
    return values * cosine[:, None, :] + turned * sine[:, None, :]


def ready_flat(raw, gain, positions):
    count = raw.shape[0]
    shaped = raw.reshape(count, -1, 128)
    return (
        rotate(head_norm(shaped, gain), positions).astype(jnp.bfloat16).reshape(count, raw.shape[1])
    )


def by_head(raw):
    return jnp.transpose(raw.reshape(raw.shape[0], -1, 128), (1, 0, 2))


def attend(running, queries, key_rows, value_rows, keep):
    total, summed = running
    scores = jnp.einsum("hqd,hkd->hqk", queries, key_rows, preferred_element_type=jnp.float32)
    weights = jnp.exp(scores) * keep[None, None, :]
    total = total + jnp.sum(weights, axis=2)
    summed = summed + jnp.einsum(
        "hqk,hkd->hqd", weights.astype(jnp.bfloat16), value_rows, preferred_element_type=jnp.float32
    )
    return (total, summed)


def local(
    image_tokens,
    modulation,
    gate,
    w_qkv,
    b_qkv,
    q_gain,
    k_gain,
    text_gain,
    w_out,
    b_out,
    text_kv,
    stale_kv,
):
    tok_rows = image_tokens.shape[0]
    own_start = lax.axis_index("patch") * tok_rows
    positions = own_start + jnp.arange(tok_rows, dtype=jnp.int32)
    prepared = jnp.stack([ready_flat(stale_kv[:, 0], k_gain, positions), stale_kv[:, 1]], axis=1)
    whole = lax.all_gather(image_tokens, "head", axis=1, tiled=True)
    inputs = whole.astype(jnp.float32)
    average = jnp.mean(inputs, axis=1, keepdims=True)
    centered = inputs - average
    spread = jnp.mean(centered * centered, axis=1, keepdims=True)
    modulated = (
        centered * lax.rsqrt(spread + 1e-06) * (1.0 + modulation[1]) + modulation[0]
    ).astype(jnp.bfloat16)
    width = w_qkv.shape[2]
    projected = jnp.dot(
        modulated, w_qkv.reshape(w_qkv.shape[0], 3 * width), preferred_element_type=jnp.float32
    )
    projected = (projected.reshape(tok_rows, 3, width) + b_qkv).astype(jnp.bfloat16)
    fresh_kv = projected[:, 1:3]
    queries = (
        rotate(head_norm(projected[:, 0].reshape(tok_rows, -1, 128), q_gain), positions)
        * 128 ** (-0.5)
    ).astype(jnp.bfloat16)
    queries = jnp.transpose(queries, (1, 0, 2))
    heads_here = queries.shape[0]
    running = (
        jnp.zeros((heads_here, tok_rows), jnp.float32),
        jnp.zeros((heads_here, tok_rows, 128), jnp.float32),
    )
    running = attend(
        running,
        queries,
        by_head(ready_flat(projected[:, 1], k_gain, positions)),
        by_head(projected[:, 2]),
        jnp.ones((tok_rows,), jnp.float32),
    )
    text_rows = text_kv.shape[0]
    text_keys = jnp.transpose(
        head_norm(text_kv[:, 0].reshape(text_rows, -1, 128), text_gain).astype(jnp.bfloat16),
        (1, 0, 2),
    )
    running = attend(
        running, queries, text_keys, by_head(text_kv[:, 1]), jnp.ones((text_rows,), jnp.float32)
    )
    piece = lax.all_gather(prepared, "patch", axis=0, tiled=True)
    count = piece.shape[0]
    places = jnp.arange(count, dtype=jnp.int32)
    keep = ((places < own_start) | (places >= own_start + tok_rows)).astype(jnp.float32)
    running = attend(running, queries, by_head(piece[:, 0]), by_head(piece[:, 1]), keep)
    total, summed = running
    attended = (
        jnp.transpose(summed / total[:, :, None], (1, 0, 2))
        .reshape(tok_rows, heads_here * 128)
        .astype(jnp.bfloat16)
    )
    partials_here = jnp.dot(attended, w_out, preferred_element_type=jnp.float32)
    branch = lax.psum_scatter(
        partials_here.astype(jnp.bfloat16), "head", scatter_dimension=1, tiled=True
    ).astype(jnp.float32)
    image_out = (image_tokens.astype(jnp.float32) + gate * (branch + b_out)).astype(jnp.bfloat16)
    return (image_out, fresh_kv)


def solution(mesh):
    in_specs = (
        P("patch", "head"),
        P(),
        P("head"),
        P(None, None, "head"),
        P(None, "head"),
        P(),
        P(),
        P(),
        P("head", None),
        P("head"),
        P(None, None, "head"),
        P("patch", None, "head"),
    )
    out_specs = (P("patch", "head"), P("patch", None, "head"))
    return jax.shard_map(local, mesh=mesh, in_specs=in_specs, out_specs=out_specs, check_vma=False)
```

profile of v0, /device:TPU:0, one launch (start us, length us, event | category | flops | bytes accessed | tf_op | source)
XLA Modules:
  0.0 459.1 jit_solution(2462048851056692571)
XLA Ops:
  8.0 4.9 %fusion.61 = (bf16[768,1,384]{2,1,0:T(2,128)(2,1)}, bf16[768,1,384]{2,1,0:T(2,128)(2,1)S(1)}) fusion(bf16[768,2,384]{2,1,0:T(2,128)(2,1)} %param.23), kind=kLoop, calls=%fused_computation.109 | loop fusion | bytes 2359296 | tf_op jit(solution)/shard_map/slice | solution.py:82
  12.8 3.3 copy.68
  16.2 10.4 %copy.43 = bf16[3072,3,384]{0,2,1:T(8,128)(2,1)} copy(bf16[3072,3,384]{2,0,1:T(8,128)(2,1)} %param.15) | data formatting | bytes 14155776 | tf_op args[3]
  27.3 3.4 copy.67
  38.6 52.9 %all-gather.3.cloned.1.call-done = bf16[768,3072]{1,0:T(8,128)(2,1)} async-done(((bf16[768,384]{1,0:T(8,128)(2,1)}), bf16[768,3072]{1,0:T(8,128)(2,1)}) %all-gather.3.cloned.1.call-update) | async-done | bytes 4718608 | tf_op jit(solution)/shard_map/all_gather | solution.py:83
  91.5 3.2 convert_reduce_fusion
  96.6 8.6 %add_convert_fusion = bf16[768,3,384]{0,2,1:T(8,128)(2,1)S(1)} fusion(bf16[3072,3,384]{0,2,1:T(8,128)(2,1)} %copy.43, bf16[768,3072]{1,0:T(8,128)(2,1)S(1)} %copy-done.1, f32[3072]{0:T(1024)S(1)} %bitcast.120, f32[3072]{0:T(1024)S(1)} %bitcast.119, f32[768]{0:T(1024)S(1)} %add_rsqrt_fusion.4, f32[768]{0:T(1024)S(1)} %broadcast_multiply_fusion, ...), kind=kOutput, calls=%fused_computation.28 | convolution fusion | flops 5451743232 | bytes 13601280 | tf_op jit(solution)/shard_map/dot_general | solution.py:92
  110.0 2.3 multiply_multiply_fusion.1
  112.3 13.0 %slice_negate_fusion = (f32[768,3,64,1]{0,3,2,1:T(1,128)S(1)}, f32[768,3,64,1]{0,3,2,1:T(1,128)S(1)}, f32[768,3,64,1]{0,3,2,1:T(1,128)}, f32[768,3,64,1]{0,3,2,1:T(1,128)}) fusion(f32[768,3,64,2]{0,3,2,1:T(2,128)S(1)} %get-tuple-element.24, f32[768,3,64,2]{0,3,2,1:T(2,128)S(1)} %get-tuple-element.23), kind=kLoop, calls=%fused_computation.60 | loop fusion | flops 294912 | bytes 4718592 | tf_op jit(solution)/shard_map/neg | solution.py:38
  125.3 2.0 pad_maximum_fusion.2
  127.4 3.0 reshape.213
  136.6 3.9 fusion.62
  140.5 3.0 copy.50
  143.4 2.9 copy.66
  148.6 2.9 reshape.215
  155.1 2.0 pad_maximum_fusion
  157.2 3.0 reshape.211
  160.2 3.4 pad_maximum_fusion.1
  163.5 3.0 reshape.212
  166.5 2.3 fusion.36
  170.5 2.0 fusion.22
  172.5 4.8 %exponential_reduce_fusion = (f32[3,768]{1,0:T(4,128)}, f32[3,768,768]{1,2,0:T(8,128)}) fusion(bf16[3,768,128]{1,2,0:T(8,128)(2,1)S(1)} %fusion.36, f32[768,3,128]{0,2,1:T(8,128)S(1)} %copy-done.11, f32[768,3,128]{0,2,1:T(8,128)S(1)} %bitcast.105, f32[128]{0:T(128)S(1)} %copy-done.29, f32[768,3]{0,1:T(4,128)S(1)} %add_rsqrt_fusion.1, ...), kind=kOutput, calls=%fused_computation.17 | convolution fusion | flops 456521472 | bytes 10832384 | tf_op jit(solution)/shard_map/hqd,hkd->hqk/dot_general | solution.py:56
  177.3 57.3 %all-gather.5.cloned.1.call-done = bf16[12288,2,384]{0,2,1:T(8,128)(2,1)} async-done(((bf16[768,2,384]{0,2,1:T(8,128)(2,1)}), bf16[12288,2,384]{0,2,1:T(8,128)(2,1)}) %all-gather.5.cloned.1.call-update) | async-done | bytes 18874384 | tf_op jit(solution)/shard_map/all_gather | solution.py:122
  234.6 14.2 %fusion.60 = (bf16[12288,1,384]{0,2,1:T(8,128)(2,1)}, bf16[12288,1,384]{0,2,1:T(8,128)(2,1)}) fusion(bf16[12288,2,384]{0,2,1:T(8,128)(2,1)} %all-gather.5.cloned.1.call-done), kind=kLoop, calls=%fused_computation.108 | loop fusion | bytes 37748736 | tf_op jit(solution)/shard_map/slice | solution.py:126
  248.8 12.7 %copy.54 = bf16[12288,3,128]{2,0,1:T(8,128)(2,1)} copy(bf16[12288,3,128]{0,2,1:T(8,128)(2,1)} %bitcast.103) | data formatting | bytes 18874368 | tf_op jit(solution)/shard_map/reshape;squeeze | solution.py:51
  261.5 42.4 %fusion = (f32[3,768]{1,0:T(4,128)S(1)}, f32[3,768,12288]{2,1,0:T(8,128)}) fusion(f32[12288]{0:T(1024)S(1)} %copy-done.2, bf16[3,768,128]{1,2,0:T(8,128)(2,1)S(1)} %copy-done.4, bf16[12288,3,128]{2,0,1:T(8,128)(2,1)} %copy.54), kind=kOutput, calls=%fused_computation.1 | convolution fusion | flops 7304378368 | bytes 123331584 | tf_op jit(solution)/shard_map/hqd,hkd->hqk/dot_general | solution.py:56
  303.9 41.3 %fusion.2 = f32[3,768,128]{1,2,0:T(8,128)} fusion(bf16[3,12288,128]{1,2,0:T(8,128)(2,1)} %bitcast.102, f32[3,768,12288]{2,1,0:T(8,128)} %get-tuple-element.30, f32[12288]{0:T(1024)S(1)} %copy-done.2), kind=kOutput, calls=%fused_computation.3 | convolution fusion | flops 7304380416 | bytes 123912192 | tf_op jit(solution)/shard_map/hqk,hkd->hqd/dot_general | solution.py:59
  345.2 5.0 %divide_convert_fusion = bf16[768,3,128]{0,2,1:T(8,128)(2,1)S(1)} fusion(f32[3,768,128]{1,2,0:T(8,128)} %fusion.2, f32[3,768,128]{1,2,0:T(8,128)} %fusion.22, bf16[3,768,128]{1,2,0:T(8,128)(2,1)S(1)} %bitcast.115, f32[3,768,768]{1,2,0:T(8,128)} %get-tuple-element.32, f32[768,3]{0,1:T(4,128)S(1)} %add_bitcast_fusion), kind=kOutput, calls=%fused_computation.44 | convolution fusion | flops 455933952 | bytes 10626048 | tf_op jit(solution)/shard_map/hqk,hkd->hqd/dot_general | solution.py:59
  350.2 4.4 convolution_convert_fusion
  354.6 6.7 %copy.64 = bf16[768,3072]{0,1:T(8,128)(2,1)} copy(bf16[768,3072]{1,0:T(8,128)(2,1)} %convolution_convert_fusion) | data formatting | bytes 9437184
  362.5 2.8 copy.56
  365.4 84.5 %reduce-scatter.4.cloned.1.call-done = bf16[384,768]{1,0:T(8,128)(2,1)} async-done(((bf16[3072,768]{1,0:T(8,128)(2,1)}), bf16[384,768]{1,0:T(8,128)(2,1)}) %reduce-scatter.4.cloned.1.call-update) | async-done | bytes 589840
  (117 shorter events, 33.4 us)
Async XLA Ops:
  7.2 343.0 %copy-start = (bf16[384,3072]{1,0:T(8,128)(2,1)S(1)}, bf16[384,3072]{1,0:T(8,128)(2,1)}, u32[]{:S(2)}) copy-start(bf16[384,3072]{1,0:T(8,128)(2,1)} %param.20) | copy-start | bytes 7077892
  7.2 84.3 %all-gather.3.cloned.1.call-start = ((), (), s32[]{:S(2)}) async-start(), calls=%async_computation.1 | async-start | bytes 5308416 | tf_op jit(solution)/shard_map/all_gather | solution.py:83
  7.9 226.7 %all-gather.5.cloned.1.call-start = ((), (), s32[]{:S(2)}) async-start(), calls=%async_computation.2 | async-start | bytes 20054016 | tf_op jit(solution)/shard_map/all_gather | solution.py:122
  16.2 10.4 %copy-start.28 = (f32[128]{0:T(128)S(1)}, f32[128]{0:T(128)}, u32[]{:S(2)}) copy-start(f32[128]{0:T(128)} %param.18) | copy-start | bytes 1540
  30.7 4.9 %copy-start.5 = (bf16[768,1,384]{0,2,1:T(8,128)(2,1)}, bf16[768,1,384]{0,2,1:T(8,128)(2,1)S(1)}, u32[]{:S(2)}) copy-start(bf16[768,1,384]{0,2,1:T(8,128)(2,1)S(1)} %copy.67) | copy-start | bytes 1769476
  35.5 3.1 copy-start.27
  91.5 3.8 copy-start.1
  95.3 1.4 copy-start.34
  105.2 1.8 copy-start.10
  108.7 1.3 copy-start.20
  131.5 1.4 copy-start.14
  135.2 314.7 %reduce-scatter.4.cloned.1.call-start = ((), (), s32[]{:S(2)}) async-start(), calls=%async_computation.3 | async-start | bytes 5308416
  151.6 2.1 copy-start.12
  151.6 2.1 copy-start.21
  166.5 2.3 copy-start.15
  166.5 2.3 copy-start.26
  166.5 2.4 copy-start.33
  168.9 3.6 copy-start.3
  168.9 1.6 copy-start.19
  170.5 2.0 copy-start.7
  170.5 2.0 copy-start.9
  170.5 2.0 copy-start.11
  170.5 2.0 copy-start.29
  248.8 12.7 %copy-start.2 = (f32[12288]{0:T(1024)S(1)}, f32[12288]{0:T(1024)}, u32[]{:S(2)}) copy-start(f32[12288]{0:T(1024)} %fusion.52) | copy-start | bytes 147460
  248.8 12.7 %copy-start.4 = (bf16[3,768,128]{1,2,0:T(8,128)(2,1)S(1)}, bf16[3,768,128]{1,2,0:T(8,128)(2,1)}, u32[]{:S(2)}) copy-start(bf16[3,768,128]{1,2,0:T(8,128)(2,1)} %copy-done.3) | copy-start | bytes 1769476
  303.9 41.3 %copy-start.24 = (f32[3,768]{1,0:T(4,128)S(1)}, f32[3,768]{1,0:T(4,128)}, u32[]{:S(2)}) copy-start(f32[3,768]{1,0:T(4,128)} %get-tuple-element.33) | copy-start | bytes 27652
  303.9 41.3 %copy-start.25 = (f32[3,768]{1,0:T(4,128)S(1)}, f32[3,768]{1,0:T(4,128)}, u32[]{:S(2)}) copy-start(f32[3,768]{1,0:T(4,128)} %get-tuple-element.31) | copy-start | bytes 27652
  303.9 41.3 %copy-start.16 = (bf16[768,1,384]{0,2,1:T(8,128)(2,1)S(1)}, bf16[768,1,384]{0,2,1:T(8,128)(2,1)}, u32[]{:S(2)}) copy-start(bf16[768,1,384]{0,2,1:T(8,128)(2,1)} %get-tuple-element.11) | copy-start | bytes 1769476
  361.3 1.3 slice-start
  365.4 85.9 %copy-start.17 = (bf16[768,384]{1,0:T(8,128)(2,1)S(1)}, bf16[768,384]{1,0:T(8,128)(2,1)}, u32[]{:S(2)}) copy-start(bf16[768,384]{1,0:T(8,128)(2,1)} %param.12) | copy-start | bytes 1769476
  365.4 85.9 %copy-start.30 = (f32[384]{0:T(512)S(1)}, f32[384]{0:T(512)}, u32[]{:S(2)}) copy-start(f32[384]{0:T(512)} %param.21) | copy-start | bytes 4612
  365.4 85.9 %copy-start.31 = (f32[384]{0:T(512)S(1)}, f32[384]{0:T(512)}, u32[]{:S(2)}) copy-start(f32[384]{0:T(512)} %param.14) | copy-start | bytes 4612
  (7 other events, 6.5 us)
Sparse Core Ops, SparseCore 0:
  10.2 81.2 all-gather.2
  135.3 99.2 all-gather.4
  361.4 88.4 reduce-scatter.3
where the time goes:
time: 463 us; the launch traced here: 459 us
  waiting for transfers between devices  195 us (42%)
  matrix products  110 us (24%)
  local copies, waits for them, and re-layouts  96.2 us (21%)
  other arithmetic  43.1 us (9%)
  between operations  14.3 us (3%)
    unnamed x4, waiting for transfers between devices  85.2 us
    all_gather x1, waiting for transfers between devices, local(): piece = lax.all_gather(prepared, 'patch', axis=0, tiled=True)  57.3 us
    all_gather x1, waiting for transfers between devices, local(): whole = lax.all_gather(image_tokens, 'head', axis=1, tiled=True)  52.9 us
    dot_general x3, matrix products, attend(): jnp.einsum('hqd,hkd->hqk', queries, key_rows, preferred_element_type=jnp....  48.7 us
    dot_general x3, matrix products, attend(): jnp.einsum('hqk,hkd->hqd', weights.astype(jnp.bfloat16), value_rows, pref...  48.2 us
    unnamed x77, local copies, waits for them, and re-layouts  35.9 us
    slice x1, local copies, waits for them, and re-layouts, local(): piece[:, 0]  14.2 us
    neg x2, other arithmetic, rotate(): -paired[..., 1]  14 us
  transfers between devices with their start and end apart: 3, of which 3 were waited for; matrix products, arithmetic and copies ran while one was open for 16% of the time, Pallas kernels for 0%

commit v1 on v0

v1 whole, which is shorter than its diff:
```python
import functools
import math

import jax
import jax.numpy as jnp
import numpy as np
from jax import lax
from jax.experimental import pallas as pl
from jax.experimental.pallas import tpu as pltpu
from jax.sharding import PartitionSpec as P

GRID_W = 256
HD = 128
VMEM_LIMIT = 56 * 1024 * 1024
BF16 = jnp.bfloat16
F32 = jnp.float32


def params():
    return pltpu.CompilerParams(vmem_limit_bytes=VMEM_LIMIT)


def vmem(count):
    return [pl.BlockSpec(memory_space=pltpu.VMEM)] * count


def cost(flops, size, exps=0):
    return pl.CostEstimate(flops=int(flops), bytes_accessed=int(size), transcendentals=int(exps))


def along_y(step):
    return [(p, ((p // 4 + step) % 4) * 4 + p % 4) for p in range(16)]


def swap_core():
    return [(p, p ^ 1) for p in range(16)]


def swap_x_lo():
    return [(p, p ^ 2) for p in range(16)]


def along_z(step):
    return [(h, ((h // 2 + step) % 4) * 2 + h % 2) for h in range(8)]


def swap_x_hi():
    return [(h, h ^ 1) for h in range(8)]


def rope_tables(own_start, tok_rows):
    lane = np.arange(HD)
    pair = lane // 2
    freq_row = np.where(
        (pair >= 8) & (pair < 36), 10000.0 ** (-2.0 * (pair - 8) / 56.0), 0.0
    ).astype(np.float32)
    freq_col = np.where(pair >= 36, 10000.0 ** (-2.0 * (pair - 36) / 56.0), 0.0).astype(np.float32)
    positions = own_start + lax.broadcasted_iota(jnp.int32, (tok_rows, HD), 0)
    grid_rows = (positions // GRID_W).astype(F32)
    grid_cols = (positions % GRID_W).astype(F32)
    angle = grid_rows * freq_row[None, :] + grid_cols * freq_col[None, :]
    sine = jnp.sin(angle)
    even = np.asarray(lane % 2 == 0)[None, :]
    return jnp.cos(angle), jnp.where(even, -sine, 0.0), jnp.where(even, 0.0, sine)


def norm_head(values, gain):
    mean = jnp.mean(values * values, axis=-1, keepdims=True)
    return values * lax.rsqrt(mean + 1e-06) * gain


def rope(values, cosine, sine_even, sine_odd):
    following = pltpu.roll(values, HD - 1, 1)
    previous = pltpu.roll(values, 1, 1)
    return values * cosine + following * sine_even + previous * sine_odd


def cached_kernel(heads, sk, sv, gain, cosine, sine_even, sine_odd, kv):
    width = heads * HD
    kv[:, width:] = sv[...]
    for h in range(heads):
        cut = slice(h * HD, (h + 1) * HD)
        normed = norm_head(sk[:, cut].astype(F32), gain[...])
        turned = rope(normed, cosine[...], sine_even[...], sine_odd[...])
        kv[:, cut] = turned.astype(BF16)


def text_kernel(heads, sk, sv, gain, kv):
    width = heads * HD
    kv[:, width:] = sv[...]
    for h in range(heads):
        cut = slice(h * HD, (h + 1) * HD)
        kv[:, cut] = norm_head(sk[:, cut].astype(F32), gain[...]).astype(BF16)


def prepare(raw_kv, gain, tables=None):
    rows, _, width = raw_kv.shape
    body = text_kernel if tables is None else cached_kernel
    operands = [raw_kv[:, 0], raw_kv[:, 1], gain.reshape(1, HD), *(tables or ())]
    return pl.pallas_call(
        functools.partial(body, width // HD),
        out_shape=jax.ShapeDtypeStruct((rows, 2 * width), BF16),
        in_specs=vmem(len(operands)),
        out_specs=pl.BlockSpec(memory_space=pltpu.VMEM),
        compiler_params=params(),
        cost_estimate=cost(30 * rows * width, 6 * rows * width * 2),
    )(*operands)


def qkv_kernel(heads, x_hi, own, partner, mod, w, bias, qg, kg, cosine, sine_even, sine_odd, *refs):
    q_out, k_out, k_raw, v_out, held, inputs, sems = refs
    ring, rows, depth = own.shape
    width = heads * HD
    features = 2 * ring * depth
    column = (x_hi[0], 1 - x_hi[0])
    copies = [
        pltpu.make_async_copy(
            w.at[j, :, column[side]],
            held.at[side, :, :, pl.ds(j * width, width)],
            sems.at[3 * side + j],
        )
        for side in range(2)
        for j in range(3)
    ]
    for copy in copies:
        copy.start()
    pieces = [(side, ref, z) for side, ref in enumerate((own, partner)) for z in range(ring)]
    total = sum(jnp.sum(ref[z].astype(F32), axis=1, keepdims=True) for _, ref, z in pieces)
    average = total * (1.0 / features)
    square = 0.0
    for _, ref, z in pieces:
        centered = ref[z].astype(F32) - average
        square = square + jnp.sum(centered * centered, axis=1, keepdims=True)
    inverse = lax.rsqrt(square * (1.0 / features) + 1e-06)
    for number, (side, ref, z) in enumerate(pieces):
        shift_scale = mod[z, column[side]]
        modulated = (ref[z].astype(F32) - average) * inverse * (
            1.0 + shift_scale[1:2]
        ) + shift_scale[0:1]
        inputs[:, number * depth : (number + 1) * depth] = modulated.astype(BF16)
    for copy in copies:
        copy.wait()
    projected = jnp.dot(
        inputs[...], held[...].reshape(features, 3 * width), preferred_element_type=F32
    )
    rounded = [
        (projected[:, j * width : (j + 1) * width] + bias[j : j + 1]).astype(BF16)
        for j in range(3)
    ]
    k_raw[...] = rounded[1]
    v_out[...] = rounded[2]
    for h in range(heads):
        cut = slice(h * HD, (h + 1) * HD)
        for source, gain, scale, out in (
            (rounded[0], qg, HD**-0.5 * math.log2(math.e), q_out),
            (rounded[1], kg, None, k_out),
        ):
            normed = norm_head(source[:, cut].astype(F32), gain[...])
            turned = rope(normed, cosine[...], sine_even[...], sine_odd[...])
            out[:, cut] = (turned if scale is None else turned * scale).astype(BF16)


def project(own, partner, chunk, x_hi, modulation, w_qkv, b_qkv, q_gain, k_gain, tables):
    ring, rows, depth = own.shape
    width = w_qkv.shape[2]
    weights = jnp.transpose(w_qkv, (1, 0, 2)).reshape(3, ring, 2, depth, width)
    shifts = jnp.transpose(modulation.reshape(2, ring, 2, depth), (1, 2, 0, 3))
    table = pl.BlockSpec((rows, HD), lambda i: (chunk, 0))
    whole = lambda *shape: pl.BlockSpec(shape, lambda i: (0,) * len(shape))
    return pl.pallas_call(
        functools.partial(qkv_kernel, width // HD),
        grid=(1,),
        in_specs=[
            pl.BlockSpec(memory_space=pltpu.SMEM),
            whole(*own.shape),
            whole(*own.shape),
            whole(*shifts.shape),
            pl.BlockSpec(memory_space=pl.ANY),
            whole(3, width),
            whole(1, HD),
            whole(1, HD),
            table,
            table,
            table,
        ],
        out_specs=[whole(rows, width)] * 4,
        out_shape=[jax.ShapeDtypeStruct((rows, width), BF16)] * 4,
        scratch_shapes=[
            pltpu.VMEM((2, ring, depth, 3 * width), BF16),
            pltpu.VMEM((rows, 2 * ring * depth), BF16),
            pltpu.SemaphoreType.DMA((6,)),
        ],
        compiler_params=params(),
        cost_estimate=cost(12 * rows * depth * ring * width, 12e6),
    )(
        x_hi,
        own,
        partner,
        shifts,
        weights,
        b_qkv,
        q_gain.reshape(1, HD),
        k_gain.reshape(1, HD),
        *tables,
    )


def attend_block(heads, q, kv, start, count, acc, den):
    width = heads * HD
    rows = pl.ds(start, count)

    def scores(h):
        return lax.dot_general(
            q[:, h * HD : (h + 1) * HD],
            kv[rows, h * HD : (h + 1) * HD],
            (((1,), (1,)), ((), ())),
            preferred_element_type=F32,
        )

    ahead = scores(0)
    for h in range(heads):
        cut = slice(h * HD, (h + 1) * HD)
        weights = jnp.exp2(ahead)
        if h + 1 < heads:
            ahead = scores(h + 1)
        den[:, cut] += sum(weights[:, c : c + HD] for c in range(0, count, HD))
        acc[:, cut] += jnp.dot(
            weights.astype(BF16),
            kv[rows, width + h * HD : width + (h + 1) * HD],
            preferred_element_type=F32,
        )


def attn_kernel(heads, layout, text, fresh, *refs):
    refs = list(refs)
    take = lambda count: [refs.pop(0) for _ in range(count)]
    (q,) = take(1)
    sources = take(sum(len(group) for group in layout))
    text_ref = take(1)[0] if text else None
    fresh_refs = take(fresh)
    packed, kv, sems, acc, den = refs
    width = heads * HD
    block = 768
    for number, group in enumerate(layout):
        offset = number * block
        for rows in group:
            pltpu.make_async_copy(
                sources.pop(0), kv.at[pl.ds(offset, rows)], sems.at[number]
            ).start()
            offset += rows
    acc[...] = jnp.zeros_like(acc)
    den[...] = jnp.zeros_like(den)
    if text:
        attend_block(heads, q, text_ref, 0, text_ref.shape[0], acc, den)
    if fresh:
        start = len(layout) * block
        rows = block * 2 // fresh
        for part in range(fresh // 2):
            here = pl.ds(start + part * rows, rows)
            kv[here, :width] = fresh_refs[2 * part][...]
            kv[here, width:] = fresh_refs[2 * part + 1][...]
        attend_block(heads, q, kv, start, block, acc, den)

    def step(i, carry):
        start = pl.multiple_of(i * block, block)
        held = kv.at[pl.ds(start, block)]
        pltpu.make_async_copy(held, held, sems.at[i]).wait()
        attend_block(heads, q, kv, start, block, acc, den)
        return carry

    lax.fori_loop(0, len(layout), step, 0)
    lane = lax.broadcasted_iota(jnp.int32, (q.shape[0], HD), 1)
    tail = jnp.zeros((q.shape[0], HD), F32)
    for h in range(heads):
        total = jnp.sum(den[:, h * HD : (h + 1) * HD], axis=1, keepdims=True)
        high = total.astype(BF16).astype(F32)
        tail = jnp.where(lane == h, high, tail)
        tail = jnp.where(lane == heads + h, total - high, tail)
    packed[:, :width] = acc[...].astype(BF16)
    packed[:, width:] = tail.astype(BF16)


def attend(q, groups, text=None, fresh=()):
    rows, width = q.shape
    heads = width // HD
    layout = tuple(tuple(part.shape[0] for part in group) for group in groups)
    flat = [part for group in groups for part in group]
    operands = [q] + flat
    specs = vmem(1) + [pl.BlockSpec(memory_space=pl.ANY)] * len(flat)
    keys = 768 * (len(groups) + bool(fresh))
    if text is not None:
        operands.append(text)
        keys += text.shape[0]
    operands.extend(fresh)
    specs.extend(vmem(len(operands) - len(specs)))
    space = 768 * (len(groups) + bool(fresh))
    return pl.pallas_call(
        functools.partial(attn_kernel, heads, layout, text is not None, len(fresh)),
        in_specs=specs,
        out_specs=pl.BlockSpec(memory_space=pltpu.VMEM),
        out_shape=jax.ShapeDtypeStruct((rows, width + HD), BF16),
        scratch_shapes=[
            pltpu.VMEM((space, 2 * width), BF16),
            pltpu.SemaphoreType.DMA((len(groups),)),
            pltpu.VMEM((rows, width), F32),
            pltpu.VMEM((rows, width), F32),
        ],
        compiler_params=params(),
        cost_estimate=cost(8 * rows * keys * width, 4 * keys * width, rows * keys * heads),
    )(*operands)


def merge_kernel(heads, here, back, w_out, out):
    width = heads * HD
    rows = here.shape[0]
    tail = here[:, width:].astype(F32) + back[:, width:].astype(F32)
    lane = lax.broadcasted_iota(jnp.int32, tail.shape, 1)
    attended = []
    for h in range(heads):
        cut = slice(h * HD, (h + 1) * HD)
        total = jnp.sum(
            jnp.where((lane == h) | (lane == heads + h), tail, 0.0), axis=1, keepdims=True
        )
        summed = here[:, cut].astype(F32) + back[:, cut].astype(F32)
        attended.append((summed / total).astype(BF16))
    attended = jnp.concatenate(attended, axis=1)
    slab = out.shape[2]
    for z in range(out.shape[0]):
        out[z] = jnp.dot(
            attended, w_out[:, z * slab : (z + 1) * slab], preferred_element_type=F32
        ).astype(BF16)


def merge(here, back, w_out):
    rows = here.shape[0]
    width, columns = w_out.shape
    return pl.pallas_call(
        functools.partial(merge_kernel, width // HD),
        out_shape=jax.ShapeDtypeStruct((4, rows, columns // 4), BF16),
        in_specs=vmem(3),
        out_specs=pl.BlockSpec(memory_space=pltpu.VMEM),
        compiler_params=params(),
        cost_estimate=cost(2 * rows * width * columns, 6e6),
    )(here, back, w_out)


def final_kernel(x_hi, image, gate, bias, *refs):
    out = refs[-1]
    chunks = len(refs) // 2
    width = image.shape[1]
    rows = image.shape[0] // chunks
    for c in range(chunks):
        cut = slice(c * rows, (c + 1) * rows)
        both, theirs = refs[2 * c : 2 * c + 2]
        own = jnp.where(x_hi[0] == 0, both[:, :width].astype(F32), both[:, width:].astype(F32))
        branch = own + theirs[...].astype(F32) + bias[...]
        out[cut] = (image[cut].astype(F32) + gate[...] * branch).astype(BF16)


def final(x_hi, image, gate, bias, pairs):
    flat = [array for pair in pairs for array in pair]
    return pl.pallas_call(
        final_kernel,
        out_shape=jax.ShapeDtypeStruct(image.shape, BF16),
        in_specs=[pl.BlockSpec(memory_space=pltpu.SMEM)] + vmem(3 + len(flat)),
        out_specs=pl.BlockSpec(memory_space=pltpu.VMEM),
        compiler_params=params(),
        cost_estimate=cost(image.size * 4, image.size * 10),
    )(x_hi, image, gate.reshape(1, -1), bias.reshape(1, -1), *flat)


def ring_gather(block, axis, move):
    half = block.shape[0] // 2
    from_minus = lax.ppermute(block, axis, move(1))
    from_plus = lax.ppermute(block, axis, move(-1))
    far_low = lax.ppermute(from_minus[:half], axis, move(1))
    far_high = lax.ppermute(from_plus[half:], axis, move(-1))
    return from_minus, from_plus, far_low, far_high


RINGS = [[0, 2, 4, 6], [1, 3, 5, 7]]


def reduce_chunk(partial, x_hi):
    both = lax.psum_scatter(
        partial, "head", scatter_dimension=0, axis_index_groups=RINGS, tiled=False
    )
    width = both.shape[1] // 2
    other = lax.dynamic_slice_in_dim(both, (1 - x_hi) * width, width, axis=1)
    return both, lax.ppermute(other, "head", swap_x_hi())


def local(
    image_tokens,
    modulation,
    gate,
    w_qkv,
    b_qkv,
    q_gain,
    k_gain,
    text_gain,
    w_out,
    b_out,
    text_kv,
    stale_kv,
):
    tok_rows = image_tokens.shape[0]
    chunks = 2
    rows = tok_rows // chunks
    patch = lax.axis_index("patch")
    x_hi = lax.axis_index("head") % 2
    side = x_hi.reshape(1).astype(jnp.int32)
    cut = lambda array, c: array[c * rows : (c + 1) * rows]
    gather_z = functools.partial(lax.all_gather, axis_name="head", axis_index_groups=RINGS)

    gathered = []
    for c in range(chunks):
        shard = cut(image_tokens, c)
        swapped = lax.ppermute(shard, "head", swap_x_hi())
        gathered.append((gather_z(shard), gather_z(swapped)))

    tables = rope_tables(patch * tok_rows, tok_rows)
    kv = prepare(stale_kv, k_gain, tables)
    text = prepare(text_kv, text_gain)
    minus, plus, low, high = ring_gather(kv, "patch", along_y)
    others = [lax.ppermute(a, "patch", swap_core()) for a in (kv, minus, plus, low, high)]
    cached = [(others[0],), (minus,), (plus,), (others[1],), (others[2],)]
    cached += [(low, high), (others[3], others[4])]

    parts = [
        project(*gathered[c], c, side, modulation, w_qkv, b_qkv, q_gain, k_gain, tables)
        for c in range(chunks)
    ]
    q_theirs = [lax.ppermute(part[0], "patch", swap_x_lo()) for part in parts]
    fresh_kv = jnp.stack(
        [jnp.concatenate([part[j] for part in parts], axis=0) for j in (2, 3)], axis=1
    )
    fresh = [array for part in parts for array in (part[1], part[3])]

    pairs = []
    q_next = q_theirs[0]
    for c in range(chunks):
        given = attend(q_next, [(kv,)] + cached)
        q_own, given = lax.optimization_barrier((parts[c][0], given))
        back = lax.ppermute(given, "patch", swap_x_lo())
        here = attend(q_own, cached, text=text, fresh=fresh)
        partial = merge(here, back, w_out)
        if c + 1 < chunks:
            q_next, partial = lax.optimization_barrier((q_theirs[c + 1], partial))
        pairs.append(reduce_chunk(partial, x_hi))
    image_out = final(side, image_tokens, gate, b_out, pairs)
    return (image_out, fresh_kv)


def solution(mesh):
    in_specs = (
        P("patch", "head"),
        P(),
        P("head"),
        P(None, None, "head"),
        P(None, "head"),
        P(),
        P(),
        P(),
        P("head", None),
        P("head"),
        P(None, None, "head"),
        P("patch", None, "head"),
    )
    out_specs = (P("patch", "head"), P("patch", None, "head"))
    return jax.shard_map(local, mesh=mesh, in_specs=in_specs, out_specs=out_specs, check_vma=False)
```

time: 463 us -> 248 us (0.54)
  matrix products: 110 us -> 0 us
  waiting for transfers between devices: 195 us -> 98.6 us
  Pallas kernels: 0 us -> 84.3 us
  local copies, waits for them, and re-layouts: 96.2 us -> 20.6 us
  other arithmetic: 43.1 us -> 4.02 us
  starting transfers between devices: 0.12 us -> 25.1 us
    dot_general x8 -> x0, matrix products: 110 us -> none  [the longest x3 48.7 us: attend(): jnp.einsum('hqd,hkd->hqk', queries, key_rows, preferred_element_type=jnp....]
    unnamed x4 -> x6, waiting for transfers between devices: 85.2 us -> 0.76 us
    pallas_call x0 -> x11, Pallas kernels: none -> 84.3 us  [the longest x4 48 us: attend(): pl.pallas_call(functools.partial(attn_kernel, heads, layout, text is not...]
    all_gather x2 -> x4, waiting for transfers between devices: 110 us -> 26.4 us  [local(): gathered.append((gather_z(shard), gather_z(swapped)))]
    ppermute x0 -> x17, waiting for transfers between devices: none -> 42.5 us  [the longest x1 15.4 us: ring_gather(): from_minus = lax.ppermute(block, axis, move(1))]
    reduce_scatter x0 -> x2, waiting for transfers between devices: none -> 29 us  [reduce_chunk(): lax.psum_scatter(partial, 'head', scatter_dimension=0, axis_index_groups=...]
    unnamed x77 -> x45, local copies, waits for them, and re-layouts: 35.9 us -> 8.27 us
    ppermute x0 -> x17, starting transfers between devices: none -> 24.9 us  [the longest x2 6.43 us: local(): swapped = lax.ppermute(shard, 'head', swap_x_hi())]
  transfers between devices with their start and end apart: 3 -> 23, of which waited for: 3 -> 8; matrix products, arithmetic and copies ran while one was open for 16% -> 7% of each run, Pallas kernels for 0% -> 33%
where the time goes in v1:
time: 248 us; the launch traced here: 247 us
  waiting for transfers between devices  98.6 us (40%)
  Pallas kernels  84.3 us (34%)
  starting transfers between devices  25.1 us (10%)
  local copies, waits for them, and re-layouts  20.6 us (8%)
  between operations  14.4 us (6%)
  other arithmetic  4.02 us (2%)
    pallas_call x4, Pallas kernels, attend(): pl.pallas_call(functools.partial(attn_kernel, heads, layout, text is not...  48 us
    reduce_scatter x2, waiting for transfers between devices, reduce_chunk(): lax.psum_scatter(partial, 'head', scatter_dimension=0, axis_index_groups=...  29 us
    all_gather x4, waiting for transfers between devices, local(): gathered.append((gather_z(shard), gather_z(swapped)))  26.4 us
    pallas_call x2, Pallas kernels, project(): pl.pallas_call(functools.partial(qkv_kernel, width // HD), grid=(1,), in_...  17.8 us
    ppermute x1, waiting for transfers between devices, ring_gather(): from_minus = lax.ppermute(block, axis, move(1))  15.4 us
    ppermute x2, waiting for transfers between devices, local(): swapped = lax.ppermute(shard, 'head', swap_x_hi())  13.1 us
    pallas_call x2, Pallas kernels, merge(): pl.pallas_call(functools.partial(merge_kernel, width // HD), out_shape=ja...  9.68 us
    ppermute x1, waiting for transfers between devices, ring_gather(): far_low = lax.ppermute(from_minus[:half], axis, move(1))  8.84 us
  transfers between devices with their start and end apart: 23, of which 8 were waited for; matrix products, arithmetic and copies ran while one was open for 7% of the time, Pallas kernels for 33%

profile of v1, /device:TPU:0, one launch (start us, length us, event | category | flops | bytes accessed | tf_op | source)
XLA Modules:
  0.0 247.1 jit_solution(14830356158106762357)
XLA Ops:
  7.2 1.9 fusion.7
  9.3 3.2 %collective-permute-start.2 = (bf16[384,384]{1,0:T(8,128)(2,1)}, bf16[384,384]{1,0:T(8,128)(2,1)S(1)}, u32[]{:S(2)}, u32[]{:S(2)}) collective-permute-start(bf16[384,384]{1,0:T(8,128)(2,1)} %get-tuple-element.36), channel_id=1, source_target_pairs={{0,1},{1,0},{2,3},{3,2},{4,5},{5,4},{6,7},{7,6},{8,9},{9,8},{10,11... | collective-permute-start | bytes 884744 | tf_op jit(solution)/shard_map/ppermute | solution.py:419
  12.4 7.2 %collective-permute-done.2 = bf16[384,384]{1,0:T(8,128)(2,1)S(1)} collective-permute-done((bf16[384,384]{1,0:T(8,128)(2,1)}, bf16[384,384]{1,0:T(8,128)(2,1)S(1)}, u32[]{:S(2)}, u32[]{:S(2)}) %collective-permute-start.2) | collective-permute-done | bytes 294944 | tf_op jit(solution)/shard_map/ppermute | solution.py:419
  21.3 3.7 %fusion.2 = (f32[768,128]{1,0:T(8,128)}, f32[768,128]{1,0:T(8,128)}, f32[768,128]{1,0:T(8,128)}) fusion(f32[128]{0:T(128)S(1)} %copy-done.16, s32[768]{0:T(1024)S(1)} %get-tuple-element.42, s32[768]{0:T(1024)S(1)} %get-tuple-element.45, f32[128]{0:T(128)S(1)} %copy-done.15, s32[768]{0:T(1024)S(1)} %get-tuple-element.41, s32[768]{0:T(1024)S(1)} %get-tuple-element.46, ...), kind=kLoop, calls=%fused_computation.11 | loop fusion | flops 983040 | bytes 1194624 | tf_op jit(solution)/shard_map/jit(_where)/select_n | solution.py:64
  25.0 1.6 fusion.5
  27.9 3.8 %shard_map.160.refs_1_ = bf16[768,768]{1,0:T(8,128)(2,1)} custom-call(bf16[768,384]{1,0:T(8,128)(2,1)} %get-tuple-element.48.sk, bf16[768,384]{1,0:T(8,128)(2,1)} %get-tuple-element.47.sv, f32[1,128]{1,0:T(1,128)} %bitcast.42, f32[768,128]{1,0:T(8,128)} %get-tuple-element.40.cosine, f32[768,128]{1,0:T(8,128)} %get-tuple-element.39.sine_even, ...), custom_call_target="tpu_custom_call" | custom-call | flops 8847360 | bytes 3538944 | tf_op jit(solution)/shard_map/pallas_call | solution.py:100
  31.6 1.8 collective-permute-start.5
  33.4 1.4 collective-permute-start.6
  34.9 3.2 %collective-permute-start = (bf16[384,384]{1,0:T(8,128)(2,1)S(1)}, bf16[384,384]{1,0:T(8,128)(2,1)S(1)}, u32[]{:S(2)}, u32[]{:S(2)}) collective-permute-start(bf16[384,384]{1,0:T(8,128)(2,1)S(1)} %copy-done.2), channel_id=1, source_target_pairs={{0,1},{1,0},{2,3},{3,2},{4,5},{5,4},{6,7},{7,6},{8,9},{9,8},{10,11... | collective-permute-start | bytes 884744 | tf_op jit(solution)/shard_map/ppermute | solution.py:419
  38.1 5.9 %collective-permute-done = bf16[384,384]{1,0:T(8,128)(2,1)S(1)} collective-permute-done((bf16[384,384]{1,0:T(8,128)(2,1)S(1)}, bf16[384,384]{1,0:T(8,128)(2,1)S(1)}, u32[]{:S(2)}, u32[]{:S(2)}) %collective-permute-start) | collective-permute-done | bytes 294944 | tf_op jit(solution)/shard_map/ppermute | solution.py:419
  44.9 15.4 %collective-permute-done.5.refs_3_.refs_2_ = bf16[768,768]{1,0:T(8,128)(2,1)} collective-permute-done((bf16[768,768]{1,0:T(8,128)(2,1)}, bf16[768,768]{1,0:T(8,128)(2,1)}, u32[]{:S(2)}, u32[]{:S(2)}) %collective-permute-start.5) | collective-permute-done | bytes 1179680 | tf_op jit(solution)/shard_map/ppermute | solution.py:374
  62.9 3.0 %collective-permute-start.10 = (bf16[384,768]{1,0:T(8,128)(2,1)S(1)}, bf16[384,768]{1,0:T(8,128)(2,1)}, u32[]{:S(2)}, u32[]{:S(2)}) collective-permute-start(bf16[384,768]{1,0:T(8,128)(2,1)S(1)} %slice.33), channel_id=1, source_target_pairs={{0,96},{8,104},{16,112},{24,120},{32,0},{40,8},{48,16},{56,24},{64... | collective-permute-start | bytes 1769480 | tf_op jit(solution)/shard_map/ppermute | solution.py:377
  67.5 8.8 %collective-permute-done.9.refs_7_.refs_6_ = bf16[384,768]{1,0:T(8,128)(2,1)} collective-permute-done((bf16[384,768]{1,0:T(8,128)(2,1)S(1)}, bf16[384,768]{1,0:T(8,128)(2,1)}, u32[]{:S(2)}, u32[]{:S(2)}) %collective-permute-start.9) | collective-permute-done | bytes 589856 | tf_op jit(solution)/shard_map/ppermute | solution.py:376
  76.8 8.9 %shard_map.159 = (bf16[384,384]{1,0:T(8,128)(2,1)}, bf16[384,384]{1,0:T(8,128)(2,1)}, bf16[384,384]{1,0:T(8,128)(2,1)}, bf16[384,384]{1,0:T(8,128)(2,1)}) custom-call(s32[1]{0:T(128)} %bitcast.x_hi, bf16[4,384,384]{2,1,0:T(8,128)(2,1)} %bitcast.37, bf16[4,384,384]{2,1,0:T(8,128)(2,1)} %bitcast.38, f32[4,2,2,384]{3,2,1,0:T(2,128)} %bitcast.40, ...), custom_call_target="tpu_custom_call" | custom-call | flops 2717908992 | bytes 12000000 | tf_op jit(solution)/shard_map/pallas_call | solution.py:170
  85.8 1.4 collective-permute-start.3
  88.2 2.3 shard_map.162.refs_10_
  90.4 26.4 %all-gather.11.cloned.1.call-done = bf16[1536,384]{1,0:T(8,128)(2,1)} async-done(((bf16[384,384]{1,0:T(8,128)(2,1)}), bf16[1536,384]{1,0:T(8,128)(2,1)}) %all-gather.11.cloned.1.call-update) | async-done | bytes 1179664 | tf_op jit(solution)/shard_map/all_gather | solution.py:420
  116.9 8.9 %shard_map.158 = (bf16[384,384]{1,0:T(8,128)(2,1)}, bf16[384,384]{1,0:T(8,128)(2,1)}, bf16[384,384]{1,0:T(8,128)(2,1)}, bf16[384,384]{1,0:T(8,128)(2,1)}) custom-call(s32[1]{0:T(128)} %bitcast.x_hi, bf16[4,384,384]{2,1,0:T(8,128)(2,1)} %bitcast.36, bf16[4,384,384]{2,1,0:T(8,128)(2,1)} %bitcast.39, f32[4,2,2,384]{3,2,1,0:T(2,128)} %bitcast.41, ...), custom_call_target="tpu_custom_call" | custom-call | flops 2717908992 | bytes 12000000 | tf_op jit(solution)/shard_map/pallas_call | solution.py:170
  125.8 1.8 collective-permute-start.1
  128.6 12.0 %shard_map.161 = bf16[384,512]{1,0:T(8,128)(2,1)} custom-call(bf16[384,384]{1,0:T(8,128)(2,1)} %copy-done.20, bf16[768,768]{1,0:T(8,128)(2,1)} %shard_map.160.refs_1_, bf16[768,768]{1,0:T(8,128)(2,1)} %collective-permute-done.4.refs_2_.refs_1_, bf16[768,768]{1,0:T(8,128)(2,1)} %collective-permute-done.5.refs_3_.refs_2_, ...), custom_call_target="tpu_custom_call" | custom-call | flops 7247757312 | bytes 9437184 | tf_op jit(solution)/shard_map/pallas_call | solution.py:297
  141.3 12.0 %shard_map.163.here = bf16[384,512]{1,0:T(8,128)(2,1)} custom-call(bf16[384,384]{1,0:T(8,128)(2,1)} %get-tuple-element.18.refs_0_, bf16[768,768]{1,0:T(8,128)(2,1)} %collective-permute-done.4.refs_2_.refs_1_, bf16[768,768]{1,0:T(8,128)(2,1)} %collective-permute-done.5.refs_3_.refs_2_, bf16[768,768]{1,0:T(8,128)(2,1)} %collective-permute-done.6.refs_4_.refs_3_, ...), custom_call_target="tpu_custom_call" | custom-call | flops 7851737088 | bytes 10223616 | tf_op jit(solution)/shard_map/pallas_call | solution.py:297
  154.0 4.8 %shard_map.164 = bf16[4,384,768]{2,1,0:T(8,128)(2,1)} custom-call(bf16[384,512]{1,0:T(8,128)(2,1)} %shard_map.163.here, bf16[384,512]{1,0:T(8,128)(2,1)} %copy-done.4, bf16[384,3072]{1,0:T(8,128)(2,1)} %w_out.3), custom_call_target="tpu_custom_call" | custom-call | flops 905969664 | bytes 6000000 | tf_op jit(solution)/shard_map/pallas_call | solution.py:337
  159.6 12.0 %shard_map.165 = bf16[384,512]{1,0:T(8,128)(2,1)} custom-call(bf16[384,384]{1,0:T(8,128)(2,1)} %copy-done.21, bf16[768,768]{1,0:T(8,128)(2,1)} %shard_map.160.refs_1_, bf16[768,768]{1,0:T(8,128)(2,1)} %collective-permute-done.4.refs_2_.refs_1_, bf16[768,768]{1,0:T(8,128)(2,1)} %collective-permute-done.5.refs_3_.refs_2_, ...), custom_call_target="tpu_custom_call" | custom-call | flops 7247757312 | bytes 9437184 | tf_op jit(solution)/shard_map/pallas_call | solution.py:297
  171.6 1.6 collective-permute-start.15
  173.1 12.0 %shard_map.166.here = bf16[384,512]{1,0:T(8,128)(2,1)} custom-call(bf16[384,384]{1,0:T(8,128)(2,1)} %get-tuple-element.26.refs_0_, bf16[768,768]{1,0:T(8,128)(2,1)} %collective-permute-done.4.refs_2_.refs_1_, bf16[768,768]{1,0:T(8,128)(2,1)} %collective-permute-done.5.refs_3_.refs_2_, bf16[768,768]{1,0:T(8,128)(2,1)} %collective-permute-done.6.refs_4_.refs_3_, ...), custom_call_target="tpu_custom_call" | custom-call | flops 7851737088 | bytes 10223616 | tf_op jit(solution)/shard_map/pallas_call | solution.py:297
  185.9 4.9 %shard_map.167 = bf16[4,384,768]{2,1,0:T(8,128)(2,1)} custom-call(bf16[384,512]{1,0:T(8,128)(2,1)} %shard_map.166.here, bf16[384,512]{1,0:T(8,128)(2,1)} %copy-done.3, bf16[384,3072]{1,0:T(8,128)(2,1)} %w_out.3), custom_call_target="tpu_custom_call" | custom-call | flops 905969664 | bytes 6000000 | tf_op jit(solution)/shard_map/pallas_call | solution.py:337
  193.7 2.7 %collective-permute-start.14 = (bf16[384,384]{1,0:T(8,128)(2,1)S(1)}, bf16[384,384]{1,0:T(8,128)(2,1)S(1)}, u32[]{:S(2)}, u32[]{:S(2)}) collective-permute-start(bf16[384,384]{1,0:T(8,128)(2,1)S(1)} %dynamic-slice_bitcast_fusion.1), channel_id=1, source_target_pairs={{0,1},{1,0},{2,3},{3,2},{4,5},{5,4},{6,7},{7,6},{8,9},{9,8},{10,11... | collective-permute-start | bytes 884744 | tf_op jit(solution)/shard_map/ppermute | solution.py:390
  196.4 29.0 %reduce-scatter.5.cloned.1.call-done = bf16[1,384,768]{2,1,0:T(8,128)(2,1)} async-done(((bf16[4,384,768]{2,1,0:T(8,128)(2,1)}), bf16[1,384,768]{2,1,0:T(8,128)(2,1)}) %reduce-scatter.5.cloned.1.call-update) | async-done | bytes 589840 | tf_op jit(solution)/shard_map/reduce_scatter | solution.py:385
  226.4 3.1 %collective-permute-start.16 = (bf16[384,384]{1,0:T(8,128)(2,1)S(1)}, bf16[384,384]{1,0:T(8,128)(2,1)S(1)}, u32[]{:S(2)}, u32[]{:S(2)}) collective-permute-start(bf16[384,384]{1,0:T(8,128)(2,1)S(1)} %dynamic-slice_bitcast_fusion), channel_id=1, source_target_pairs={{0,1},{1,0},{2,3},{3,2},{4,5},{5,4},{6,7},{7,6},{8,9},{9,8},{10,11... | collective-permute-start | bytes 884744 | tf_op jit(solution)/shard_map/ppermute | solution.py:390
  229.7 2.2 copy.21
  232.0 4.8 %collective-permute-done.16.refs_3_ = bf16[384,384]{1,0:T(8,128)(2,1)S(1)} collective-permute-done((bf16[384,384]{1,0:T(8,128)(2,1)S(1)}, bf16[384,384]{1,0:T(8,128)(2,1)S(1)}, u32[]{:S(2)}, u32[]{:S(2)}) %collective-permute-start.16) | collective-permute-done | bytes 294944 | tf_op jit(solution)/shard_map/ppermute | solution.py:390
  237.5 2.8 %shard_map.168 = bf16[768,384]{1,0:T(8,128)(2,1)} custom-call(s32[1]{0:T(128)} %bitcast.x_hi, bf16[768,384]{1,0:T(8,128)(2,1)} %image.1, f32[1,384]{1,0:T(1,128)} %reshape.36.gate, f32[1,384]{1,0:T(1,128)} %reshape.37.bias, bf16[384,768]{1,0:T(8,128)(2,1)} %bitcast.34, bf16[384,384]{1,0:T(8,128)(2,1)} %copy-done.11, bf16[384,768]{1,0:T(8,128)(2,1)} %bitcast.35, ...), custom_call_target="tpu_custom_call" | custom-call | flops 1179648 | bytes 2949120 | tf_op jit(solution)/shard_map/pallas_call | solution.py:362
  (94 shorter events, 18.2 us)
Async XLA Ops:
  7.2 14.1 %copy-start.15 = (f32[128]{0:T(128)S(1)}, f32[128]{0:T(128)}, u32[]{:S(2)}) copy-start(f32[128]{0:T(128)} %constant.71) | copy-start | bytes 1540
  7.2 14.1 %copy-start.16 = (f32[128]{0:T(128)S(1)}, f32[128]{0:T(128)}, u32[]{:S(2)}) copy-start(f32[128]{0:T(128)} %constant.72) | copy-start | bytes 1540
  7.2 14.1 %copy-start.17 = (pred[128]{0:T(512)(128)(4,1)S(1)}, pred[128]{0:T(512)(128)(4,1)}, u32[]{:S(2)}) copy-start(pred[128]{0:T(512)(128)(4,1)} %constant.73) | copy-start | bytes 388
  7.2 69.6 %all-gather.13.cloned.1.call-start = ((), (), s32[]{:S(2)}) async-start(), calls=%async_computation.6 | async-start | bytes 1474560 | tf_op jit(solution)/shard_map/all_gather | solution.py:420
  9.2 15.8 %copy-start = (bf16[768,2,384]{2,1,0:T(2,128)(2,1)S(1)}, bf16[768,2,384]{2,1,0:T(2,128)(2,1)}, u32[]{:S(2)}) copy-start(bf16[768,2,384]{2,1,0:T(2,128)(2,1)} %param.26) | copy-start | bytes 3538948
  9.2 67.6 %all-gather.15.cloned.1.call-start = ((), (), s32[]{:S(2)}) async-start(), calls=%async_computation.7 | async-start | bytes 1474560 | tf_op jit(solution)/shard_map/all_gather | solution.py:420
  9.3 10.4 %collective-permute-start.2 = (bf16[384,384]{1,0:T(8,128)(2,1)}, bf16[384,384]{1,0:T(8,128)(2,1)S(1)}, u32[]{:S(2)}, u32[]{:S(2)}) collective-permute-start(bf16[384,384]{1,0:T(8,128)(2,1)} %get-tuple-element.36), channel_id=1, source_target_pairs={{0,1},{1,0},{2,3},{3,2},{4,5},{5,4},{6,7},{7,6},{8,9},{9,8},{10,11... | collective-permute-start | bytes 884744 | tf_op jit(solution)/shard_map/ppermute | solution.py:419
  20.4 70.0 %all-gather.9.cloned.1.call-start = ((), (), s32[]{:S(2)}) async-start(), calls=%async_computation.4 | async-start | bytes 1474560 | tf_op jit(solution)/shard_map/all_gather | solution.py:420
  21.1 95.7 %all-gather.11.cloned.1.call-start = ((), (), s32[]{:S(2)}) async-start(), calls=%async_computation.5 | async-start | bytes 1474560 | tf_op jit(solution)/shard_map/all_gather | solution.py:420
  31.6 28.6 %collective-permute-start.5 = (bf16[768,768]{1,0:T(8,128)(2,1)}, bf16[768,768]{1,0:T(8,128)(2,1)}, u32[]{:S(2)}, u32[]{:S(2)}) collective-permute-start(bf16[768,768]{1,0:T(8,128)(2,1)} %shard_map.160.refs_1_), channel_id=1, source_target_pairs={{0,32},{8,40},{16,48},{24,56},{32,64},{40,72},{48,80},{56,88},{64,... | collective-permute-start | bytes 3538952 | tf_op jit(solution)/shard_map/ppermute | solution.py:374
  33.4 28.3 %collective-permute-start.6 = (bf16[768,768]{1,0:T(8,128)(2,1)}, bf16[768,768]{1,0:T(8,128)(2,1)}, u32[]{:S(2)}, u32[]{:S(2)}) collective-permute-start(bf16[768,768]{1,0:T(8,128)(2,1)} %shard_map.160.refs_1_), channel_id=1, source_target_pairs={{0,96},{8,104},{16,112},{24,120},{32,0},{40,8},{48,16},{56,24},{64... | collective-permute-start | bytes 3538952 | tf_op jit(solution)/shard_map/ppermute | solution.py:375
  34.9 9.1 %collective-permute-start = (bf16[384,384]{1,0:T(8,128)(2,1)S(1)}, bf16[384,384]{1,0:T(8,128)(2,1)S(1)}, u32[]{:S(2)}, u32[]{:S(2)}) collective-permute-start(bf16[384,384]{1,0:T(8,128)(2,1)S(1)} %copy-done.2), channel_id=1, source_target_pairs={{0,1},{1,0},{2,3},{3,2},{4,5},{5,4},{6,7},{7,6},{8,9},{9,8},{10,11... | collective-permute-start | bytes 884744 | tf_op jit(solution)/shard_map/ppermute | solution.py:419
  44.7 21.7 %copy-start.1 = (bf16[512,2,384]{2,1,0:T(2,128)(2,1)S(1)}, bf16[512,2,384]{2,1,0:T(2,128)(2,1)}, u32[]{:S(2)}) copy-start(bf16[512,2,384]{2,1,0:T(2,128)(2,1)} %param.25) | copy-start | bytes 2359300
  44.7 147.9 %reduce-scatter.3.cloned.1.call-start = ((), (), s32[]{:S(2)}) async-start(), calls=%async_computation.2 | async-start | bytes 2949120 | tf_op jit(solution)/shard_map/reduce_scatter | solution.py:385
  44.8 41.0 %collective-permute-start.4 = (bf16[768,768]{1,0:T(8,128)(2,1)}, bf16[768,768]{1,0:T(8,128)(2,1)}, u32[]{:S(2)}, u32[]{:S(2)}) collective-permute-start(bf16[768,768]{1,0:T(8,128)(2,1)} %shard_map.160.refs_1_), channel_id=1, source_target_pairs={{0,8},{8,0},{16,24},{24,16},{32,40},{40,32},{48,56},{56,48},{64,72... | collective-permute-start | bytes 3538952 | tf_op jit(solution)/shard_map/ppermute | solution.py:426
  61.4 14.9 %collective-permute-start.9 = (bf16[384,768]{1,0:T(8,128)(2,1)S(1)}, bf16[384,768]{1,0:T(8,128)(2,1)}, u32[]{:S(2)}, u32[]{:S(2)}) collective-permute-start(bf16[384,768]{1,0:T(8,128)(2,1)S(1)} %slice.32), channel_id=1, source_target_pairs={{0,32},{8,40},{16,48},{24,56},{32,64},{40,72},{48,80},{56,88},{64,... | collective-permute-start | bytes 1769480 | tf_op jit(solution)/shard_map/ppermute | solution.py:376
  62.9 13.8 %collective-permute-start.10 = (bf16[384,768]{1,0:T(8,128)(2,1)S(1)}, bf16[384,768]{1,0:T(8,128)(2,1)}, u32[]{:S(2)}, u32[]{:S(2)}) collective-permute-start(bf16[384,768]{1,0:T(8,128)(2,1)S(1)} %slice.33), channel_id=1, source_target_pairs={{0,96},{8,104},{16,112},{24,120},{32,0},{40,8},{48,16},{56,24},{64... | collective-permute-start | bytes 1769480 | tf_op jit(solution)/shard_map/ppermute | solution.py:377
  65.9 61.7 %collective-permute-start.7 = (bf16[768,768]{1,0:T(8,128)(2,1)}, bf16[768,768]{1,0:T(8,128)(2,1)}, u32[]{:S(2)}, u32[]{:S(2)}) collective-permute-start(bf16[768,768]{1,0:T(8,128)(2,1)} %collective-permute-done.5.refs_3_.refs_2_), channel_id=1, source_target_pairs={{0,8},{8,0},{16,24},{24,16},{32,40},{40,32},{48,56},{56,48},{64,72... | collective-permute-start | bytes 3538952 | tf_op jit(solution)/shard_map/ppermute | solution.py:426
  65.9 61.8 %collective-permute-start.8 = (bf16[768,768]{1,0:T(8,128)(2,1)}, bf16[768,768]{1,0:T(8,128)(2,1)}, u32[]{:S(2)}, u32[]{:S(2)}) collective-permute-start(bf16[768,768]{1,0:T(8,128)(2,1)} %collective-permute-done.6.refs_4_.refs_3_), channel_id=1, source_target_pairs={{0,8},{8,0},{16,24},{24,16},{32,40},{40,32},{48,56},{56,48},{64,72... | collective-permute-start | bytes 3538952 | tf_op jit(solution)/shard_map/ppermute | solution.py:426
  76.3 51.3 %collective-permute-start.11 = (bf16[384,768]{1,0:T(8,128)(2,1)}, bf16[384,768]{1,0:T(8,128)(2,1)S(1)}, u32[]{:S(2)}, u32[]{:S(2)}) collective-permute-start(bf16[384,768]{1,0:T(8,128)(2,1)} %collective-permute-done.9.refs_7_.refs_6_), channel_id=1, source_target_pairs={{0,8},{8,0},{16,24},{24,16},{32,40},{40,32},{48,56},{56,48},{64,72... | collective-permute-start | bytes 1769480 | tf_op jit(solution)/shard_map/ppermute | solution.py:426
  76.7 50.9 %collective-permute-start.12 = (bf16[384,768]{1,0:T(8,128)(2,1)}, bf16[384,768]{1,0:T(8,128)(2,1)S(1)}, u32[]{:S(2)}, u32[]{:S(2)}) collective-permute-start(bf16[384,768]{1,0:T(8,128)(2,1)} %collective-permute-done.10.refs_8_.refs_7_), channel_id=1, source_target_pairs={{0,8},{8,0},{16,24},{24,16},{32,40},{40,32},{48,56},{56,48},{64,72... | collective-permute-start | bytes 1769480 | tf_op jit(solution)/shard_map/ppermute | solution.py:426
  85.8 40.0 %collective-permute-start.3 = (bf16[384,384]{1,0:T(8,128)(2,1)}, bf16[384,384]{1,0:T(8,128)(2,1)S(1)}, u32[]{:S(2)}, u32[]{:S(2)}) collective-permute-start(bf16[384,384]{1,0:T(8,128)(2,1)} %get-tuple-element.18.refs_0_), channel_id=1, source_target_pairs={{0,16},{8,24},{16,0},{24,8},{32,48},{40,56},{48,32},{56,40},{64,80... | collective-permute-start | bytes 884744 | tf_op jit(solution)/shard_map/ppermute | solution.py:434
  125.8 33.0 %collective-permute-start.1 = (bf16[384,384]{1,0:T(8,128)(2,1)}, bf16[384,384]{1,0:T(8,128)(2,1)S(1)}, u32[]{:S(2)}, u32[]{:S(2)}) collective-permute-start(bf16[384,384]{1,0:T(8,128)(2,1)} %get-tuple-element.26.refs_0_), channel_id=1, source_target_pairs={{0,16},{8,24},{16,0},{24,8},{32,48},{40,56},{48,32},{56,40},{64,80... | collective-permute-start | bytes 884744 | tf_op jit(solution)/shard_map/ppermute | solution.py:434
  140.7 12.6 %collective-permute-start.13 = (bf16[384,512]{1,0:T(8,128)(2,1)}, bf16[384,512]{1,0:T(8,128)(2,1)S(1)}, u32[]{:S(2)}, u32[]{:S(2)}) collective-permute-start(bf16[384,512]{1,0:T(8,128)(2,1)} %shard_map.161), channel_id=1, source_target_pairs={{0,16},{8,24},{16,0},{24,8},{32,48},{40,56},{48,32},{56,40},{64,80... | collective-permute-start | bytes 1179656 | tf_op jit(solution)/shard_map/ppermute | solution.py:445
  159.5 65.8 %reduce-scatter.5.cloned.1.call-start = ((), (), s32[]{:S(2)}) async-start(), calls=%async_computation.3 | async-start | bytes 2949120 | tf_op jit(solution)/shard_map/reduce_scatter | solution.py:385
  171.6 13.5 %collective-permute-start.15 = (bf16[384,512]{1,0:T(8,128)(2,1)}, bf16[384,512]{1,0:T(8,128)(2,1)S(1)}, u32[]{:S(2)}, u32[]{:S(2)}) collective-permute-start(bf16[384,512]{1,0:T(8,128)(2,1)} %shard_map.165), channel_id=1, source_target_pairs={{0,16},{8,24},{16,0},{24,8},{32,48},{40,56},{48,32},{56,40},{64,80... | collective-permute-start | bytes 1179656 | tf_op jit(solution)/shard_map/ppermute | solution.py:445
  190.8 38.6 %copy-start.8 = (bf16[384,384]{1,0:T(8,128)(2,1)S(1)}, bf16[384,384]{1,0:T(8,128)(2,1)}, u32[]{:S(2)}) copy-start(bf16[384,384]{1,0:T(8,128)(2,1)} %get-tuple-element.20.refs_12_) | copy-start | bytes 884740
  190.8 38.6 %copy-start.10 = (bf16[384,384]{1,0:T(8,128)(2,1)S(1)}, bf16[384,384]{1,0:T(8,128)(2,1)}, u32[]{:S(2)}) copy-start(bf16[384,384]{1,0:T(8,128)(2,1)} %get-tuple-element.22.refs_14_) | copy-start | bytes 884740
  192.6 36.9 %copy-start.7 = (bf16[384,384]{1,0:T(8,128)(2,1)S(1)}, bf16[384,384]{1,0:T(8,128)(2,1)}, u32[]{:S(2)}) copy-start(bf16[384,384]{1,0:T(8,128)(2,1)} %get-tuple-element.28) | copy-start | bytes 884740
  192.6 36.9 %copy-start.9 = (bf16[384,384]{1,0:T(8,128)(2,1)S(1)}, bf16[384,384]{1,0:T(8,128)(2,1)}, u32[]{:S(2)}) copy-start(bf16[384,384]{1,0:T(8,128)(2,1)} %get-tuple-element.29) | copy-start | bytes 884740
  193.7 38.3 %collective-permute-start.14 = (bf16[384,384]{1,0:T(8,128)(2,1)S(1)}, bf16[384,384]{1,0:T(8,128)(2,1)S(1)}, u32[]{:S(2)}, u32[]{:S(2)}) collective-permute-start(bf16[384,384]{1,0:T(8,128)(2,1)S(1)} %dynamic-slice_bitcast_fusion.1), channel_id=1, source_target_pairs={{0,1},{1,0},{2,3},{3,2},{4,5},{5,4},{6,7},{7,6},{8,9},{9,8},{10,11... | collective-permute-start | bytes 884744 | tf_op jit(solution)/shard_map/ppermute | solution.py:390
  226.4 10.4 %collective-permute-start.16 = (bf16[384,384]{1,0:T(8,128)(2,1)S(1)}, bf16[384,384]{1,0:T(8,128)(2,1)S(1)}, u32[]{:S(2)}, u32[]{:S(2)}) collective-permute-start(bf16[384,384]{1,0:T(8,128)(2,1)S(1)} %dynamic-slice_bitcast_fusion), channel_id=1, source_target_pairs={{0,1},{1,0},{2,3},{3,2},{4,5},{5,4},{6,7},{7,6},{8,9},{9,8},{10,11... | collective-permute-start | bytes 884744 | tf_op jit(solution)/shard_map/ppermute | solution.py:390
  (13 other events, 21.8 us)
Sparse Core Ops, SparseCore 0:
  9.7 27.0 all-gather.12
  38.5 25.0 all-gather.14
  65.2 25.0 all-gather.8
  91.8 25.0 all-gather.10
  159.0 32.4 reduce-scatter.2
  193.7 31.6 reduce-scatter.4

commit v2 on v1

v2 whole, which is shorter than its diff:
```python
import functools
import math

import jax
import jax.numpy as jnp
import numpy as np
from jax import lax
from jax.experimental import pallas as pl
from jax.experimental.pallas import tpu as pltpu
from jax.sharding import PartitionSpec as P

GRID_W = 256
HD = 128
VMEM_LIMIT = 56 * 1024 * 1024
BF16 = jnp.bfloat16
F32 = jnp.float32


def params():
    return pltpu.CompilerParams(vmem_limit_bytes=VMEM_LIMIT)


def vmem(count):
    return [pl.BlockSpec(memory_space=pltpu.VMEM)] * count


def cost(flops, size, exps=0):
    return pl.CostEstimate(flops=int(flops), bytes_accessed=int(size), transcendentals=int(exps))


def along_y(step):
    return [(p, ((p // 4 + step) % 4) * 4 + p % 4) for p in range(16)]


def swap_core():
    return [(p, p ^ 1) for p in range(16)]


def swap_x_lo():
    return [(p, p ^ 2) for p in range(16)]


def along_z(step):
    return [(h, ((h // 2 + step) % 4) * 2 + h % 2) for h in range(8)]


def swap_x_hi():
    return [(h, h ^ 1) for h in range(8)]


def rope_tables(own_start, tok_rows):
    lane = np.arange(HD)
    pair = lane // 2
    freq_row = np.where(
        (pair >= 8) & (pair < 36), 10000.0 ** (-2.0 * (pair - 8) / 56.0), 0.0
    ).astype(np.float32)
    freq_col = np.where(pair >= 36, 10000.0 ** (-2.0 * (pair - 36) / 56.0), 0.0).astype(np.float32)
    positions = own_start + lax.broadcasted_iota(jnp.int32, (tok_rows, HD), 0)
    grid_rows = (positions // GRID_W).astype(F32)
    grid_cols = (positions % GRID_W).astype(F32)
    angle = grid_rows * freq_row[None, :] + grid_cols * freq_col[None, :]
    sine = jnp.sin(angle)
    even = np.asarray(lane % 2 == 0)[None, :]
    return jnp.cos(angle), jnp.where(even, -sine, 0.0), jnp.where(even, 0.0, sine)


def norm_head(values, gain):
    mean = jnp.mean(values * values, axis=-1, keepdims=True)
    return values * lax.rsqrt(mean + 1e-06) * gain


def rope(values, cosine, sine_even, sine_odd):
    following = pltpu.roll(values, HD - 1, 1)
    previous = pltpu.roll(values, 1, 1)
    return values * cosine + following * sine_even + previous * sine_odd


def cached_kernel(heads, sk, sv, gain, cosine, sine_even, sine_odd, kv):
    width = heads * HD
    kv[:, width:] = sv[...]
    for h in range(heads):
        cut = slice(h * HD, (h + 1) * HD)
        normed = norm_head(sk[:, cut].astype(F32), gain[...])
        turned = rope(normed, cosine[...], sine_even[...], sine_odd[...])
        kv[:, cut] = turned.astype(BF16)


def text_kernel(heads, sk, sv, gain, kv):
    width = heads * HD
    kv[:, width:] = sv[...]
    for h in range(heads):
        cut = slice(h * HD, (h + 1) * HD)
        kv[:, cut] = norm_head(sk[:, cut].astype(F32), gain[...]).astype(BF16)


def prepare(raw_kv, gain, tables=None):
    rows, _, width = raw_kv.shape
    body = text_kernel if tables is None else cached_kernel
    operands = [raw_kv[:, 0], raw_kv[:, 1], gain.reshape(1, HD), *(tables or ())]
    return pl.pallas_call(
        functools.partial(body, width // HD),
        out_shape=jax.ShapeDtypeStruct((rows, 2 * width), BF16),
        in_specs=vmem(len(operands)),
        out_specs=pl.BlockSpec(memory_space=pltpu.VMEM),
        compiler_params=params(),
        cost_estimate=cost(30 * rows * width, 6 * rows * width * 2),
    )(*operands)


def qkv_kernel(heads, blocks, ids, *refs):
    pieces = refs[:blocks]
    mod, w, bias, qg, kg, cosine, sine_even, sine_odd = refs[blocks : blocks + 8]
    q_out, k_out, k_raw, v_out, held, inputs, sems = refs[blocks + 8 :]
    rows, depth = pieces[0].shape
    width = heads * HD
    features = blocks * depth
    copies = [
        pltpu.make_async_copy(
            w.at[j, ids[b]], held.at[b, :, pl.ds(j * width, width)], sems.at[3 * b + j]
        )
        for b in range(blocks)
        for j in range(3)
    ]

    @pl.when(pl.program_id(0) == 0)
    def _():
        for copy in copies:
            copy.start()

    total = sum(jnp.sum(ref[...].astype(F32), axis=1, keepdims=True) for ref in pieces)
    average = total * (1.0 / features)
    square = 0.0
    for ref in pieces:
        centered = ref[...].astype(F32) - average
        square = square + jnp.sum(centered * centered, axis=1, keepdims=True)
    inverse = lax.rsqrt(square * (1.0 / features) + 1e-06)
    for b, ref in enumerate(pieces):
        shift_scale = mod[ids[b]]
        modulated = (ref[...].astype(F32) - average) * inverse * (
            1.0 + shift_scale[1:2]
        ) + shift_scale[0:1]
        inputs[:, b * depth : (b + 1) * depth] = modulated.astype(BF16)

    @pl.when(pl.program_id(0) == 0)
    def _():
        for copy in copies:
            copy.wait()

    projected = jnp.dot(
        inputs[...], held[...].reshape(features, 3 * width), preferred_element_type=F32
    )
    rounded = [
        (projected[:, j * width : (j + 1) * width] + bias[j : j + 1]).astype(BF16)
        for j in range(3)
    ]
    k_raw[...] = rounded[1]
    v_out[...] = rounded[2]
    for h in range(heads):
        cut = slice(h * HD, (h + 1) * HD)
        for source, gain, scale, out in (
            (rounded[0], qg, HD**-0.5 * math.log2(math.e), q_out),
            (rounded[1], kg, None, k_out),
        ):
            normed = norm_head(source[:, cut].astype(F32), gain[...])
            turned = rope(normed, cosine[...], sine_even[...], sine_odd[...])
            out[:, cut] = (turned if scale is None else turned * scale).astype(BF16)


def project(pieces, ids, modulation, w_qkv, b_qkv, q_gain, k_gain, tables):
    blocks = len(pieces)
    rows, depth = pieces[0].shape
    width = w_qkv.shape[2]
    tile = rows // 2
    weights = jnp.transpose(w_qkv, (1, 0, 2)).reshape(3, blocks, depth, width)
    shifts = jnp.transpose(modulation.reshape(2, blocks, depth), (1, 0, 2))
    whole = lambda *shape: pl.BlockSpec(shape, lambda i: (0,) * len(shape))
    part = lambda columns: pl.BlockSpec((tile, columns), lambda i: (i, 0))
    return pl.pallas_call(
        functools.partial(qkv_kernel, width // HD, blocks),
        grid=(rows // tile,),
        in_specs=[pl.BlockSpec(memory_space=pltpu.SMEM)]
        + [part(depth)] * blocks
        + [
            whole(*shifts.shape),
            pl.BlockSpec(memory_space=pl.ANY),
            whole(3, width),
            whole(1, HD),
            whole(1, HD),
            part(HD),
            part(HD),
            part(HD),
        ],
        out_specs=[part(width)] * 4,
        out_shape=[jax.ShapeDtypeStruct((rows, width), BF16)] * 4,
        scratch_shapes=[
            pltpu.VMEM((blocks, depth, 3 * width), BF16),
            pltpu.VMEM((tile, blocks * depth), BF16),
            pltpu.SemaphoreType.DMA((3 * blocks,)),
        ],
        compiler_params=params(),
        cost_estimate=cost(6 * rows * depth * blocks * width, 15e6),
    )(
        ids,
        *pieces,
        shifts,
        weights,
        b_qkv,
        q_gain.reshape(1, HD),
        k_gain.reshape(1, HD),
        *tables,
    )


def attend_keys(heads, q, places, acc, den):
    width = heads * HD
    steps = [(place, h) for place in places for h in range(heads)]

    def scores(step):
        (ref, start, count), h = step
        return lax.dot_general(
            q[:, h * HD : (h + 1) * HD],
            ref[pl.ds(start, count), h * HD : (h + 1) * HD],
            (((1,), (1,)), ((), ())),
            preferred_element_type=F32,
        )

    ahead = scores(steps[0])
    for number, ((ref, start, count), h) in enumerate(steps):
        cut = slice(h * HD, (h + 1) * HD)
        weights = jnp.exp2(ahead)
        if number + 1 < len(steps):
            ahead = scores(steps[number + 1])
        den[:, cut] += sum(weights[:, c : c + HD] for c in range(0, count, HD))
        acc[:, cut] += jnp.dot(
            weights.astype(BF16),
            ref[pl.ds(start, count), width + h * HD : width + (h + 1) * HD],
            preferred_element_type=F32,
        )


def attn_kernel(heads, layout, text, tile, unroll, *refs):
    refs = list(refs)
    q = refs.pop(0)
    sources = [refs.pop(0) for group in layout for _ in group]
    text_ref = refs.pop(0) if text else None
    packed, kv, sems, acc, den = refs
    width = heads * HD
    block = 768
    for number, group in enumerate(layout):
        for first, rows, lane, lanes in group:
            pltpu.make_async_copy(
                sources.pop(0),
                kv.at[pl.ds(number * block + first, rows), pl.ds(lane, lanes)],
                sems.at[number],
            ).start()
    acc[...] = jnp.zeros_like(acc)
    den[...] = jnp.zeros_like(den)
    if text:
        count = text_ref.shape[0]
        cut = min(tile, count)
        attend_keys(heads, q, [(text_ref, c, cut) for c in range(0, count, cut)], acc, den)

    def step(i, carry):
        places = []
        for u in range(unroll):
            start = pl.multiple_of((i * unroll + u) * block, block)
            held = kv.at[pl.ds(start, block)]
            pltpu.make_async_copy(held, held, sems.at[i * unroll + u]).wait()
            places += [(kv, start + c, tile) for c in range(0, block, tile)]
        attend_keys(heads, q, places, acc, den)
        return carry

    lax.fori_loop(0, len(layout) // unroll, step, 0)
    lane = lax.broadcasted_iota(jnp.int32, (q.shape[0], HD), 1)
    tail = jnp.zeros((q.shape[0], HD), F32)
    for h in range(heads):
        total = jnp.sum(den[:, h * HD : (h + 1) * HD], axis=1, keepdims=True)
        high = total.astype(BF16).astype(F32)
        tail = jnp.where(lane == h, high, tail)
        tail = jnp.where(lane == heads + h, total - high, tail)
    packed[:, :width] = acc[...].astype(BF16)
    packed[:, width:] = tail.astype(BF16)


def attend(q, groups, text=None, tile=768, unroll=1):
    rows, width = q.shape
    heads = width // HD
    layout = tuple(
        tuple((first, part.shape[0], lane, part.shape[1]) for part, first, lane in group)
        for group in groups
    )
    flat = [part for group in groups for part, _, _ in group]
    operands = [q] + flat
    specs = vmem(1) + [pl.BlockSpec(memory_space=pl.ANY)] * len(flat)
    keys = 768 * len(groups)
    if text is not None:
        operands.append(text)
        specs += vmem(1)
        keys += text.shape[0]
    return pl.pallas_call(
        functools.partial(attn_kernel, heads, layout, text is not None, tile, unroll),
        in_specs=specs,
        out_specs=pl.BlockSpec(memory_space=pltpu.VMEM),
        out_shape=jax.ShapeDtypeStruct((rows, width + HD), BF16),
        scratch_shapes=[
            pltpu.VMEM((768 * len(groups), 2 * width), BF16),
            pltpu.SemaphoreType.DMA((len(groups),)),
            pltpu.VMEM((rows, width), F32),
            pltpu.VMEM((rows, width), F32),
        ],
        compiler_params=params(),
        cost_estimate=cost(8 * rows * keys * width, 4 * keys * width, rows * keys * heads),
    )(*operands)


def attended_rows(heads, here, back):
    width = heads * HD
    tail = here[:, width:].astype(F32) + back[:, width:].astype(F32)
    lane = lax.broadcasted_iota(jnp.int32, tail.shape, 1)
    attended = []
    for h in range(heads):
        cut = slice(h * HD, (h + 1) * HD)
        total = jnp.sum(
            jnp.where((lane == h) | (lane == heads + h), tail, 0.0), axis=1, keepdims=True
        )
        summed = here[:, cut].astype(F32) + back[:, cut].astype(F32)
        attended.append((summed / total).astype(BF16))
    return jnp.concatenate(attended, axis=1)


def merge_kernel(heads, here, back, w_out, out):
    attended = attended_rows(heads, here, back)
    slab = out.shape[2]
    for z in range(out.shape[0]):
        out[z] = jnp.dot(
            attended, w_out[:, z * slab : (z + 1) * slab], preferred_element_type=F32
        ).astype(BF16)


def merge_ring_kernel(heads, z, here, back, w_out, *outs):
    attended = attended_rows(heads, here, back)
    slab = outs[0].shape[1]
    for dz, out in enumerate(outs):
        first = pl.multiple_of(lax.rem(z[0] + dz, len(outs)) * slab, slab)
        out[...] = jnp.dot(
            attended, w_out[:, pl.ds(first, slab)], preferred_element_type=F32
        ).astype(BF16)


def merge(here, back, w_out, z=None):
    rows = here.shape[0]
    width, columns = w_out.shape
    if z is None:
        body, first, specs = merge_kernel, (), []
        out_shape = jax.ShapeDtypeStruct((8, rows, columns // 8), BF16)
        out_specs = pl.BlockSpec(memory_space=pltpu.VMEM)
    else:
        body, first, specs = merge_ring_kernel, (z,), [pl.BlockSpec(memory_space=pltpu.SMEM)]
        out_shape = [jax.ShapeDtypeStruct((rows, columns // 4), BF16)] * 4
        out_specs = vmem(4)
    return pl.pallas_call(
        functools.partial(body, width // HD),
        out_shape=out_shape,
        in_specs=specs + vmem(3),
        out_specs=out_specs,
        compiler_params=params(),
        cost_estimate=cost(2 * rows * width * columns, 6e6),
    )(*first, here, back, w_out)


def join_kernel(x_hi, a, b, c, d, mine, other):
    width = mine.shape[1]
    total = sum(ref[...].astype(F32) for ref in (a, b, c, d))
    low, high = total[:, :width], total[:, width:]
    mine[...] = jnp.where(x_hi[0] == 0, low, high)
    other[...] = jnp.where(x_hi[0] == 0, high, low).astype(BF16)


def join(x_hi, slabs):
    rows, both = slabs[0].shape
    return pl.pallas_call(
        join_kernel,
        out_shape=[
            jax.ShapeDtypeStruct((rows, both // 2), F32),
            jax.ShapeDtypeStruct((rows, both // 2), BF16),
        ],
        in_specs=[pl.BlockSpec(memory_space=pltpu.SMEM)] + vmem(4),
        out_specs=vmem(2),
        compiler_params=params(),
        cost_estimate=cost(rows * both * 4, rows * both * 12),
    )(x_hi, *slabs)


def final_kernel(image, gate, bias, mine, theirs, sent, out):
    rows = mine.shape[0]
    branches = (
        mine[...] + theirs[...].astype(F32),
        sum(sent[h].astype(F32) for h in range(sent.shape[0])),
    )
    for c, branch in enumerate(branches):
        cut = slice(c * rows, (c + 1) * rows)
        out[cut] = (image[cut].astype(F32) + gate[...] * (branch + bias[...])).astype(BF16)


def final(image, gate, bias, mine, theirs, sent):
    return pl.pallas_call(
        final_kernel,
        out_shape=jax.ShapeDtypeStruct(image.shape, BF16),
        in_specs=vmem(6),
        out_specs=pl.BlockSpec(memory_space=pltpu.VMEM),
        compiler_params=params(),
        cost_estimate=cost(image.size * 4, image.size * 10),
    )(image, gate.reshape(1, -1), bias.reshape(1, -1), mine, theirs, sent)


def local(
    image_tokens,
    modulation,
    gate,
    w_qkv,
    b_qkv,
    q_gain,
    k_gain,
    text_gain,
    w_out,
    b_out,
    text_kv,
    stale_kv,
):
    tok_rows, width = image_tokens.shape
    chunks = 2
    rows = tok_rows // chunks
    patch = lax.axis_index("patch")
    head = lax.axis_index("head")
    x_hi = head % 2
    z_here = (head // 2).reshape(1).astype(jnp.int32)
    side = x_hi.reshape(1).astype(jnp.int32)
    cut = lambda array, c: array[c * rows : (c + 1) * rows]
    to_z = lambda array, step: lax.ppermute(array, "head", along_z(step))
    to_x = lambda array: lax.ppermute(array, "head", swap_x_hi())
    to_y = lambda array, step: lax.ppermute(array, "patch", along_y(step))

    partner = to_x(image_tokens)
    near = [image_tokens, to_z(image_tokens, 1), to_z(image_tokens, -1), to_z(image_tokens, 2)]
    table = [
        [((h // 2 + dz) % 4) * 2 + (h + dx) % 2 for dx in range(2) for dz in (0, 3, 1, 2)]
        for h in range(8)
    ]
    ids = lax.dynamic_index_in_dim(jnp.asarray(table, jnp.int32), head, 0, keepdims=False)

    tables = rope_tables(patch * tok_rows, tok_rows)
    kv = prepare(stale_kv, k_gain, tables)
    partner, kv = lax.optimization_barrier((partner, kv))
    column = [kv, to_y(kv, 1), to_y(kv, -1)]
    near[1], near[2], partner = lax.optimization_barrier((near[1], near[2], partner))
    far = [partner, to_z(partner, 1), to_z(partner, -1), to_x(near[3])]
    far, column = lax.optimization_barrier((far, column))
    column += [to_y(cut(column[1], 0), 1), to_y(cut(column[2], 1), -1)]
    text = prepare(text_kv, text_gain)
    single = lambda array: [(array, 0, 0)]

    q, k_fresh, k_raw, values = project(
        near + far, ids, modulation, w_qkv, b_qkv, q_gain, k_gain, tables
    )
    q, column = lax.optimization_barrier((q, column))
    swapped = [lax.ppermute(a, "patch", swap_core()) for a in column]
    cached = [single(a) for a in swapped[:1] + column[1:3] + swapped[1:3]]
    cached += [[(low, 0, 0), (high, rows, 0)] for low, high in (column[3:], swapped[3:])]
    fresh_kv = jnp.stack([k_raw, values], axis=1)
    fresh = [(k_fresh, 0, 0), (values, 0, width)]
    q_theirs = [lax.ppermute(cut(q, c), "patch", swap_x_lo()) for c in range(chunks)]

    outputs = []
    q_next = q_theirs[0]
    for c in range(chunks):
        tile, unroll = ((768, 2), (256, 1))[c]
        given = attend(q_next, [single(kv)] + cached, tile=tile, unroll=unroll)
        if c == 1:
            given, *arrived = lax.optimization_barrier((given, *arrived))
            mine, other = join(side, [slabs[0], *arrived])
            theirs = to_x(other)
        q_own, given = lax.optimization_barrier((cut(q, c), given))
        back = lax.ppermute(given, "patch", swap_x_lo())
        here = attend(q_own, [fresh] + cached, text=text, tile=tile, unroll=unroll)
        if c == 0:
            slabs = merge(here, back, w_out, z_here)
            q_next, slabs = lax.optimization_barrier((q_theirs[1], slabs))
            arrived = [to_z(slabs[dz], dz) for dz in range(1, 4)]
        else:
            sent = lax.all_to_all(merge(here, back, w_out), "head", 0, 0, tiled=True)
    image_out = final(image_tokens, gate, b_out, mine, theirs, sent)
    return (image_out, fresh_kv)


def solution(mesh):
    in_specs = (
        P("patch", "head"),
        P(),
        P("head"),
        P(None, None, "head"),
        P(None, "head"),
        P(),
        P(),
        P(),
        P("head", None),
        P("head"),
        P(None, None, "head"),
        P("patch", None, "head"),
    )
    out_specs = (P("patch", "head"), P("patch", None, "head"))
    return jax.shard_map(local, mesh=mesh, in_specs=in_specs, out_specs=out_specs, check_vma=False)
```

time: 248 us -> 220 us (0.89)
  waiting for transfers between devices: 98.6 us -> 68.9 us
  between operations: 14.4 us -> 0.97 us
  starting transfers between devices: 25.1 us -> 37.2 us
  Pallas kernels: 84.3 us -> 89.3 us
    reduce_scatter x2 -> x0, waiting for transfers between devices: 29 us -> none  [reduce_chunk(): lax.psum_scatter(partial, 'head', scatter_dimension=0, axis_index_groups=...]
    ppermute x15 -> x22, waiting for transfers between devices: 42.5 us -> 68.9 us  [the longest x8 31 us: local(): to_z = lambda array, step: lax.ppermute(array, 'head', along_z(step))]
    all_gather x4 -> x0, waiting for transfers between devices: 26.4 us -> none  [local(): gathered.append((gather_z(shard), gather_z(swapped)))]
    ppermute x15 -> x22, starting transfers between devices: 22.7 us -> 29.5 us  [the longest x8 13.7 us: local(): to_z = lambda array, step: lax.ppermute(array, 'head', along_z(step))]
    all_to_all x0 -> x1, starting transfers between devices: none -> 5.35 us  [local(): sent = lax.all_to_all(merge(here, back, w_out), 'head', 0, 0, tiled=True)]
    unnamed x45 -> x49, local copies, waits for them, and re-layouts: 8.27 us -> 6.73 us
  transfers between devices with their start and end apart: 23 -> 25, of which waited for: 8 -> 7; matrix products, arithmetic and copies ran while one was open for 7% -> 8% of each run, Pallas kernels for 33% -> 37%
where the time goes in v2:
time: 220 us; the launch traced here: 219 us
  Pallas kernels  89.3 us (41%)
  waiting for transfers between devices  68.9 us (31%)
  starting transfers between devices  37.2 us (17%)
  local copies, waits for them, and re-layouts  18.9 us (9%)
  other arithmetic  3.86 us (2%)
    pallas_call x4, Pallas kernels, attend(): pl.pallas_call(functools.partial(attn_kernel, heads, layout, text is not...  50.3 us
    ppermute x8, waiting for transfers between devices, local(): to_z = lambda array, step: lax.ppermute(array, 'head', along_z(step))  31 us
    ppermute x3, waiting for transfers between devices, local(): to_x = lambda array: lax.ppermute(array, 'head', swap_x_hi())  29.3 us
    pallas_call x1, Pallas kernels, project(): pl.pallas_call(functools.partial(qkv_kernel, width // HD, blocks), grid=(...  17.3 us
    ppermute x8, starting transfers between devices, local(): to_z = lambda array, step: lax.ppermute(array, 'head', along_z(step))  13.7 us
    pallas_call x2, Pallas kernels, merge(): pl.pallas_call(functools.partial(body, width // HD), out_shape=out_shape,...  9.21 us
    ppermute x2, waiting for transfers between devices, local(): lax.ppermute(cut(q, c), 'patch', swap_x_lo())  8.6 us
    ppermute x3, starting transfers between devices, local(): to_x = lambda array: lax.ppermute(array, 'head', swap_x_hi())  7.2 us
  transfers between devices with their start and end apart: 25, of which 7 were waited for; matrix products, arithmetic and copies ran while one was open for 8% of the time, Pallas kernels for 37%

profile of v2, /device:TPU:0, one launch (start us, length us, event | category | flops | bytes accessed | tf_op | source)
XLA Modules:
  0.0 219.2 jit_solution(9484780698073988211)
XLA Ops:
  0.6 3.2 %collective-permute-start.2 = (bf16[768,384]{1,0:T(8,128)(2,1)}, bf16[768,384]{1,0:T(8,128)(2,1)S(1)}, u32[]{:S(2)}, u32[]{:S(2)}) collective-permute-start(bf16[768,384]{1,0:T(8,128)(2,1)} %image.1), channel_id=1, source_target_pairs={{0,1},{1,0},{2,3},{3,2},{4,5},{5,4},{6,7},{7,6},{8,9},{9,8},{10,11... | collective-permute-start | bytes 1769480 | tf_op jit(solution)/shard_map/ppermute | solution.py:440
  3.8 1.9 collective-permute-start
  5.7 2.1 collective-permute-start.1
  7.9 1.9 collective-permute-start.3
  9.8 3.7 %fusion.5 = (bf16[768,1,384]{2,1,0:T(2,128)(2,1)S(1)}, bf16[768,1,384]{2,1,0:T(2,128)(2,1)S(1)}) fusion(bf16[768,2,384]{2,1,0:T(2,128)(2,1)} %param.27), kind=kLoop, calls=%fused_computation.22 | loop fusion | bytes 2359296 | tf_op jit(solution)/shard_map/slice | solution.py:99
  13.5 3.7 %fusion.2 = (f32[768,128]{1,0:T(8,128)}, f32[768,128]{1,0:T(8,128)}, f32[768,128]{1,0:T(8,128)}) fusion(f32[128]{0:T(128)S(1)} %copy-done.16, s32[768]{0:T(1024)S(1)} %get-tuple-element.98, s32[768]{0:T(1024)S(1)} %get-tuple-element.101, f32[128]{0:T(128)S(1)} %copy-done.15, s32[768]{0:T(1024)S(1)} %get-tuple-element.97, s32[768]{0:T(1024)S(1)} %get-tuple-element.102, ...), kind=kLoop, calls=%fused_computation.9 | loop fusion | flops 983040 | bytes 1194624 | tf_op jit(solution)/shard_map/jit(_where)/select_n | solution.py:64
  18.5 3.7 %shard_map.167.refs_1_ = bf16[768,768]{1,0:T(8,128)(2,1)} custom-call(bf16[768,384]{1,0:T(8,128)(2,1)} %get-tuple-element.96.sk, bf16[768,384]{1,0:T(8,128)(2,1)} %get-tuple-element.95.sv, f32[1,128]{1,0:T(1,128)} %bitcast.26, f32[768,128]{1,0:T(8,128)} %get-tuple-element.94.cosine.refs_13_, f32[768,128]{1,0:T(8,128)} %get-tuple-element.93.sine_even.refs_14_, ...), custom_call_target="tpu_custom_call" | custom-call | flops 8847360 | bytes 3538944 | tf_op jit(solution)/shard_map/pallas_call | solution.py:100
  22.2 1.6 collective-permute-start.7
  23.7 1.7 collective-permute-start.8
  25.4 7.5 %collective-permute-done.1.refs_2_ = bf16[768,384]{1,0:T(8,128)(2,1)S(1)} collective-permute-done((bf16[768,384]{1,0:T(8,128)(2,1)}, bf16[768,384]{1,0:T(8,128)(2,1)S(1)}, u32[]{:S(2)}, u32[]{:S(2)}) %collective-permute-start.1) | collective-permute-done | bytes 589856 | tf_op jit(solution)/shard_map/ppermute | solution.py:439
  32.9 4.1 %collective-permute-start.5 = (bf16[768,384]{1,0:T(8,128)(2,1)S(1)}, bf16[768,384]{1,0:T(8,128)(2,1)}, u32[]{:S(2)}, u32[]{:S(2)}) collective-permute-start(bf16[768,384]{1,0:T(8,128)(2,1)S(1)} %collective-permute-done.2.refs_4_), channel_id=1, source_target_pairs={{0,6},{1,7},{2,0},{3,1},{4,2},{5,3},{6,4},{7,5},{8,14},{9,15},{10,... | collective-permute-start | bytes 1769480 | tf_op jit(solution)/shard_map/ppermute | solution.py:439
  37.5 10.2 %collective-permute-done.4.refs_5_ = bf16[768,384]{1,0:T(8,128)(2,1)} collective-permute-done((bf16[768,384]{1,0:T(8,128)(2,1)S(1)}, bf16[768,384]{1,0:T(8,128)(2,1)}, u32[]{:S(2)}, u32[]{:S(2)}) %collective-permute-start.4) | collective-permute-done | bytes 589856 | tf_op jit(solution)/shard_map/ppermute | solution.py:439
  47.7 3.1 %collective-permute-done.6.refs_7_ = bf16[768,384]{1,0:T(8,128)(2,1)} collective-permute-done((bf16[768,384]{1,0:T(8,128)(2,1)}, bf16[768,384]{1,0:T(8,128)(2,1)}, u32[]{:S(2)}, u32[]{:S(2)}) %collective-permute-start.6) | collective-permute-done | bytes 589856 | tf_op jit(solution)/shard_map/ppermute | solution.py:440
  52.3 3.1 %collective-permute-start.10 = (bf16[384,768]{1,0:T(8,128)(2,1)S(1)}, bf16[384,768]{1,0:T(8,128)(2,1)}, u32[]{:S(2)}, u32[]{:S(2)}) collective-permute-start(bf16[384,768]{1,0:T(8,128)(2,1)S(1)} %slice.29), channel_id=1, source_target_pairs={{0,96},{8,104},{16,112},{24,120},{32,0},{40,8},{48,16},{56,24},{64... | collective-permute-start | bytes 1769480 | tf_op jit(solution)/shard_map/ppermute | solution.py:441
  57.0 17.3 %shard_map.168 = (bf16[768,384]{1,0:T(8,128)(2,1)}, bf16[768,384]{1,0:T(8,128)(2,1)}, bf16[768,384]{1,0:T(8,128)(2,1)}, bf16[768,384]{1,0:T(8,128)(2,1)}) custom-call(s32[8]{0:T(128)} %dynamic-slice_bitcast_fusion.ids, bf16[768,384]{1,0:T(8,128)(2,1)} %image.1, bf16[768,384]{1,0:T(8,128)(2,1)} %copy-done.19, bf16[768,384]{1,0:T(8,128)(2,1)} %copy-done.20, ...), custom_call_target="tpu_custom_call" | custom-call | flops 5435817984 | bytes 15000000 | tf_op jit(solution)/shard_map/pallas_call | solution.py:178
  77.6 8.6 %collective-permute-done.12.refs_0_ = bf16[384,384]{1,0:T(8,128)(2,1)S(1)} collective-permute-done((bf16[384,384]{1,0:T(8,128)(2,1)S(1)}, bf16[384,384]{1,0:T(8,128)(2,1)S(1)}, u32[]{:S(2)}, u32[]{:S(2)}) %collective-permute-start.12) | collective-permute-done | bytes 294944 | tf_op jit(solution)/shard_map/ppermute | solution.py:471
  89.0 2.3 %shard_map.170.refs_12_ = bf16[512,768]{1,0:T(8,128)(2,1)} custom-call(bf16[512,384]{1,0:T(8,128)(2,1)} %get-tuple-element.104.sk, bf16[512,384]{1,0:T(8,128)(2,1)} %get-tuple-element.103.sv, f32[1,128]{1,0:T(1,128)} %bitcast.25), custom_call_target="tpu_custom_call" | custom-call | flops 5898240 | bytes 2359296 | tf_op jit(solution)/shard_map/pallas_call | solution.py:100
  92.0 12.1 %shard_map.169 = bf16[384,512]{1,0:T(8,128)(2,1)} custom-call(bf16[384,384]{1,0:T(8,128)(2,1)} %copy-done.22, bf16[768,768]{1,0:T(8,128)(2,1)} %shard_map.167.refs_1_, bf16[768,768]{1,0:T(8,128)(2,1)} %collective-permute-done.13.refs_2_.refs_3_, bf16[768,768]{1,0:T(8,128)(2,1)} %copy-done.10, bf16[768,768]{1,0:T(8,128)(2,1)} %collective-permute-done.8.refs_4_.refs_5_, ...), custom_call_target="tpu_custom_call" | custom-call | flops 7247757312 | bytes 9437184 | tf_op jit(solution)/shard_map/pallas_call | solution.py:300
  104.1 1.7 collective-permute-start.18
  105.8 12.3 %shard_map.171.here = bf16[384,512]{1,0:T(8,128)(2,1)} custom-call(bf16[384,384]{1,0:T(8,128)(2,1)} %copy-done.12, bf16[768,384]{1,0:T(8,128)(2,1)} %get-tuple-element.63.refs_1_, bf16[768,384]{1,0:T(8,128)(2,1)} %get-tuple-element.64.refs_2_, bf16[768,768]{1,0:T(8,128)(2,1)} %collective-permute-done.13.refs_2_.refs_3_, bf16[768,768]{1,0:T(8,128)(2,1)} %copy-done.10, ...), custom_call_target="tpu_custom_call" | custom-call | flops 7851737088 | bytes 10223616 | tf_op jit(solution)/shard_map/pallas_call | solution.py:300
  118.9 4.2 %shard_map.172 = (bf16[384,768]{1,0:T(8,128)(2,1)}, bf16[384,768]{1,0:T(8,128)(2,1)}, bf16[384,768]{1,0:T(8,128)(2,1)}, bf16[384,768]{1,0:T(8,128)(2,1)}) custom-call(s32[1]{0:T(128)} %bitcast.10.z, bf16[384,512]{1,0:T(8,128)(2,1)} %shard_map.171.here, bf16[384,512]{1,0:T(8,128)(2,1)} %copy-done.21, bf16[384,3072]{1,0:T(8,128)(2,1)} %w_out.3), custom_call_target="tpu_custom_call" | custom-call | flops 905969664 | bytes 6000000 | tf_op jit(solution)/shard_map/pallas_call | solution.py:361
  124.0 1.6 collective-permute-start.20
  126.9 12.8 %shard_map.173 = bf16[384,512]{1,0:T(8,128)(2,1)} custom-call(bf16[384,384]{1,0:T(8,128)(2,1)} %copy-done.23, bf16[768,768]{1,0:T(8,128)(2,1)} %shard_map.167.refs_1_, bf16[768,768]{1,0:T(8,128)(2,1)} %collective-permute-done.13.refs_2_.refs_3_, bf16[768,768]{1,0:T(8,128)(2,1)} %copy-done.10, bf16[768,768]{1,0:T(8,128)(2,1)} %collective-permute-done.8.refs_4_.refs_5_, ...), custom_call_target="tpu_custom_call" | custom-call | flops 7247757312 | bytes 9437184 | tf_op jit(solution)/shard_map/pallas_call | solution.py:300
  139.7 12.7 %collective-permute-done.19.b = bf16[384,768]{1,0:T(8,128)(2,1)S(1)} collective-permute-done((bf16[384,768]{1,0:T(8,128)(2,1)}, bf16[384,768]{1,0:T(8,128)(2,1)S(1)}, u32[]{:S(2)}, u32[]{:S(2)}) %collective-permute-start.19) | collective-permute-done | bytes 589856 | tf_op jit(solution)/shard_map/ppermute | solution.py:439
  153.6 13.1 %shard_map.175.here = bf16[384,512]{1,0:T(8,128)(2,1)} custom-call(bf16[384,384]{1,0:T(8,128)(2,1)} %copy-done.11, bf16[768,384]{1,0:T(8,128)(2,1)} %get-tuple-element.63.refs_1_, bf16[768,384]{1,0:T(8,128)(2,1)} %get-tuple-element.64.refs_2_, bf16[768,768]{1,0:T(8,128)(2,1)} %collective-permute-done.13.refs_2_.refs_3_, bf16[768,768]{1,0:T(8,128)(2,1)} %copy-done.10, ...), custom_call_target="tpu_custom_call" | custom-call | flops 7851737088 | bytes 10223616 | tf_op jit(solution)/shard_map/pallas_call | solution.py:300
  167.6 5.0 %shard_map.176 = bf16[8,384,384]{2,1,0:T(8,128)(2,1)} custom-call(bf16[384,512]{1,0:T(8,128)(2,1)} %shard_map.175.here, bf16[384,512]{1,0:T(8,128)(2,1)} %copy-done.8, bf16[384,3072]{1,0:T(8,128)(2,1)} %w_out.3), custom_call_target="tpu_custom_call" | custom-call | flops 905969664 | bytes 6000000 | tf_op jit(solution)/shard_map/pallas_call | solution.py:361
  172.6 5.4 %all-to-all-start = ((bf16[8,384,384]{2,1,0:T(8,128)(2,1)}), bf16[8,384,384]{2,1,0:T(8,128)(2,1)S(1)}, u32[]{:S(2)}, u32[]{:S(2)}) async-start(bf16[8,384,384]{2,1,0:T(8,128)(2,1)} %shard_map.176), calls=%async_computation | async-start | bytes 4718592 | tf_op jit(solution)/shard_map/all_to_all | solution.py:490
  178.0 3.0 %shard_map.174 = (f32[384,384]{1,0:T(8,128)}, bf16[384,384]{1,0:T(8,128)(2,1)}) custom-call(s32[1]{0:T(128)} %bitcast.x_hi, bf16[384,768]{1,0:T(8,128)(2,1)} %get-tuple-element.70.a, bf16[384,768]{1,0:T(8,128)(2,1)} %copy-done.3, bf16[384,768]{1,0:T(8,128)(2,1)} %copy-done.4, bf16[384,768]{1,0:T(8,128)(2,1)} %copy-done.5), custom_call_target="tpu_custom_call" | custom-call | flops 1179648 | bytes 3538944 | tf_op jit(solution)/shard_map/pallas_call | solution.py:381
  180.9 3.5 %collective-permute-start.22 = (bf16[384,384]{1,0:T(8,128)(2,1)}, bf16[384,384]{1,0:T(8,128)(2,1)S(1)}, u32[]{:S(2)}, u32[]{:S(2)}) collective-permute-start(bf16[384,384]{1,0:T(8,128)(2,1)} %get-tuple-element.79), channel_id=1, source_target_pairs={{0,1},{1,0},{2,3},{3,2},{4,5},{5,4},{6,7},{7,6},{8,9},{9,8},{10,11... | collective-permute-start | bytes 884744 | tf_op jit(solution)/shard_map/ppermute | solution.py:440
  185.8 2.2 %copy.22 = bf16[768,2,384]{2,1,0:T(2,128)(2,1)} copy(bf16[768,2,384]{2,0,1:T(8,128)(2,1)S(1)} %pad_maximum_fusion) | data formatting | bytes 2359296
  188.0 26.2 %collective-permute-done.22.theirs = bf16[384,384]{1,0:T(8,128)(2,1)S(1)} collective-permute-done((bf16[384,384]{1,0:T(8,128)(2,1)}, bf16[384,384]{1,0:T(8,128)(2,1)S(1)}, u32[]{:S(2)}, u32[]{:S(2)}) %collective-permute-start.22) | collective-permute-done | bytes 294944 | tf_op jit(solution)/shard_map/ppermute | solution.py:440
  215.7 3.5 %shard_map.177 = bf16[768,384]{1,0:T(8,128)(2,1)} custom-call(bf16[768,384]{1,0:T(8,128)(2,1)} %image.1, f32[1,384]{1,0:T(1,128)} %reshape.32.gate, f32[1,384]{1,0:T(1,128)} %reshape.33.bias, f32[384,384]{1,0:T(8,128)} %get-tuple-element.78.mine, bf16[384,384]{1,0:T(8,128)(2,1)} %copy-done.9, bf16[8,384,384]{2,1,0:T(8,128)(2,1)} %copy-done), custom_call_target="tpu_custom_call" | custom-call | flops 1179648 | bytes 2949120 | tf_op jit(solution)/shard_map/pallas_call | solution.py:406
  (93 shorter events, 19.3 us)
Async XLA Ops:
  0.6 21.5 %collective-permute-start.2 = (bf16[768,384]{1,0:T(8,128)(2,1)}, bf16[768,384]{1,0:T(8,128)(2,1)S(1)}, u32[]{:S(2)}, u32[]{:S(2)}) collective-permute-start(bf16[768,384]{1,0:T(8,128)(2,1)} %image.1), channel_id=1, source_target_pairs={{0,1},{1,0},{2,3},{3,2},{4,5},{5,4},{6,7},{7,6},{8,9},{9,8},{10,11... | collective-permute-start | bytes 1769480 | tf_op jit(solution)/shard_map/ppermute | solution.py:440
  3.8 21.6 %collective-permute-start = (bf16[768,384]{1,0:T(8,128)(2,1)}, bf16[768,384]{1,0:T(8,128)(2,1)S(1)}, u32[]{:S(2)}, u32[]{:S(2)}) collective-permute-start(bf16[768,384]{1,0:T(8,128)(2,1)} %image.1), channel_id=1, source_target_pairs={{0,2},{1,3},{2,4},{3,5},{4,6},{5,7},{6,0},{7,1},{8,10},{9,11},{10,... | collective-permute-start | bytes 1769480 | tf_op jit(solution)/shard_map/ppermute | solution.py:439
  5.7 27.1 %collective-permute-start.1 = (bf16[768,384]{1,0:T(8,128)(2,1)}, bf16[768,384]{1,0:T(8,128)(2,1)S(1)}, u32[]{:S(2)}, u32[]{:S(2)}) collective-permute-start(bf16[768,384]{1,0:T(8,128)(2,1)} %image.1), channel_id=1, source_target_pairs={{0,6},{1,7},{2,0},{3,1},{4,2},{5,3},{6,4},{7,5},{8,14},{9,15},{10,... | collective-permute-start | bytes 1769480 | tf_op jit(solution)/shard_map/ppermute | solution.py:439
  7.9 29.1 %collective-permute-start.3 = (bf16[768,384]{1,0:T(8,128)(2,1)}, bf16[768,384]{1,0:T(8,128)(2,1)}, u32[]{:S(2)}, u32[]{:S(2)}) collective-permute-start(bf16[768,384]{1,0:T(8,128)(2,1)} %image.1), channel_id=1, source_target_pairs={{0,4},{1,5},{2,6},{3,7},{4,0},{5,1},{6,2},{7,3},{8,12},{9,13},{10,... | collective-permute-start | bytes 1769480 | tf_op jit(solution)/shard_map/ppermute | solution.py:439
  22.2 33.3 %copy-start.18 = (bf16[768,384]{1,0:T(8,128)(2,1)}, bf16[768,384]{1,0:T(8,128)(2,1)S(1)}, u32[]{:S(2)}) copy-start(bf16[768,384]{1,0:T(8,128)(2,1)S(1)} %collective-permute-done.2.refs_4_) | copy-start | bytes 1769476
  22.2 28.6 %collective-permute-start.7 = (bf16[768,768]{1,0:T(8,128)(2,1)}, bf16[768,768]{1,0:T(8,128)(2,1)S(1)}, u32[]{:S(2)}, u32[]{:S(2)}) collective-permute-start(bf16[768,768]{1,0:T(8,128)(2,1)} %shard_map.167.refs_1_), channel_id=1, source_target_pairs={{0,32},{8,40},{16,48},{24,56},{32,64},{40,72},{48,80},{56,88},{64,... | collective-permute-start | bytes 3538952 | tf_op jit(solution)/shard_map/ppermute | solution.py:441
  23.7 27.0 %collective-permute-start.8 = (bf16[768,768]{1,0:T(8,128)(2,1)}, bf16[768,768]{1,0:T(8,128)(2,1)}, u32[]{:S(2)}, u32[]{:S(2)}) collective-permute-start(bf16[768,768]{1,0:T(8,128)(2,1)} %shard_map.167.refs_1_), channel_id=1, source_target_pairs={{0,96},{8,104},{16,112},{24,120},{32,0},{40,8},{48,16},{56,24},{64... | collective-permute-start | bytes 3538952 | tf_op jit(solution)/shard_map/ppermute | solution.py:441
  25.4 30.0 %copy-start.19 = (bf16[768,384]{1,0:T(8,128)(2,1)}, bf16[768,384]{1,0:T(8,128)(2,1)S(1)}, u32[]{:S(2)}) copy-start(bf16[768,384]{1,0:T(8,128)(2,1)S(1)} %collective-permute-done.refs_1_) | copy-start | bytes 1769476
  32.9 22.6 %copy-start.20 = (bf16[768,384]{1,0:T(8,128)(2,1)}, bf16[768,384]{1,0:T(8,128)(2,1)S(1)}, u32[]{:S(2)}) copy-start(bf16[768,384]{1,0:T(8,128)(2,1)S(1)} %collective-permute-done.1.refs_2_) | copy-start | bytes 1769476
  32.9 14.8 %collective-permute-start.4 = (bf16[768,384]{1,0:T(8,128)(2,1)S(1)}, bf16[768,384]{1,0:T(8,128)(2,1)}, u32[]{:S(2)}, u32[]{:S(2)}) collective-permute-start(bf16[768,384]{1,0:T(8,128)(2,1)S(1)} %collective-permute-done.2.refs_4_), channel_id=1, source_target_pairs={{0,2},{1,3},{2,4},{3,5},{4,6},{5,7},{6,0},{7,1},{8,10},{9,11},{10,... | collective-permute-start | bytes 1769480 | tf_op jit(solution)/shard_map/ppermute | solution.py:439
  32.9 14.8 %collective-permute-start.5 = (bf16[768,384]{1,0:T(8,128)(2,1)S(1)}, bf16[768,384]{1,0:T(8,128)(2,1)}, u32[]{:S(2)}, u32[]{:S(2)}) collective-permute-start(bf16[768,384]{1,0:T(8,128)(2,1)S(1)} %collective-permute-done.2.refs_4_), channel_id=1, source_target_pairs={{0,6},{1,7},{2,0},{3,1},{4,2},{5,3},{6,4},{7,5},{8,14},{9,15},{10,... | collective-permute-start | bytes 1769480 | tf_op jit(solution)/shard_map/ppermute | solution.py:439
  37.0 13.8 %collective-permute-start.6 = (bf16[768,384]{1,0:T(8,128)(2,1)}, bf16[768,384]{1,0:T(8,128)(2,1)}, u32[]{:S(2)}, u32[]{:S(2)}) collective-permute-start(bf16[768,384]{1,0:T(8,128)(2,1)} %collective-permute-done.3.refs_3_), channel_id=1, source_target_pairs={{0,1},{1,0},{2,3},{3,2},{4,5},{5,4},{6,7},{7,6},{8,9},{9,8},{10,11... | collective-permute-start | bytes 1769480 | tf_op jit(solution)/shard_map/ppermute | solution.py:440
  50.8 23.7 %copy-start.10 = (bf16[768,768]{1,0:T(8,128)(2,1)}, bf16[768,768]{1,0:T(8,128)(2,1)S(1)}, u32[]{:S(2)}) copy-start(bf16[768,768]{1,0:T(8,128)(2,1)S(1)} %collective-permute-done.7.refs_3_.refs_4_) | copy-start | bytes 3538948
  52.3 22.0 %collective-permute-start.10 = (bf16[384,768]{1,0:T(8,128)(2,1)S(1)}, bf16[384,768]{1,0:T(8,128)(2,1)}, u32[]{:S(2)}, u32[]{:S(2)}) collective-permute-start(bf16[384,768]{1,0:T(8,128)(2,1)S(1)} %slice.29), channel_id=1, source_target_pairs={{0,96},{8,104},{16,112},{24,120},{32,0},{40,8},{48,16},{56,24},{64... | collective-permute-start | bytes 1769480 | tf_op jit(solution)/shard_map/ppermute | solution.py:441
  55.5 18.9 %collective-permute-start.9 = (bf16[384,768]{1,0:T(8,128)(2,1)S(1)}, bf16[384,768]{1,0:T(8,128)(2,1)}, u32[]{:S(2)}, u32[]{:S(2)}) collective-permute-start(bf16[384,768]{1,0:T(8,128)(2,1)S(1)} %slice.28), channel_id=1, source_target_pairs={{0,32},{8,40},{16,48},{24,56},{32,64},{40,72},{48,80},{56,88},{64,... | collective-permute-start | bytes 1769480 | tf_op jit(solution)/shard_map/ppermute | solution.py:441
  57.0 17.3 %copy-start.2 = (bf16[768,768]{1,0:T(8,128)(2,1)S(1)}, bf16[768,768]{1,0:T(8,128)(2,1)}, u32[]{:S(2)}) copy-start(bf16[768,768]{1,0:T(8,128)(2,1)} %shard_map.167.refs_1_) | copy-start | bytes 3538948
  74.4 17.6 %collective-permute-start.13 = (bf16[768,768]{1,0:T(8,128)(2,1)S(1)}, bf16[768,768]{1,0:T(8,128)(2,1)}, u32[]{:S(2)}, u32[]{:S(2)}) collective-permute-start(bf16[768,768]{1,0:T(8,128)(2,1)S(1)} %copy-done.2), channel_id=1, source_target_pairs={{0,8},{8,0},{16,24},{24,16},{32,40},{40,32},{48,56},{56,48},{64,72... | collective-permute-start | bytes 3538952 | tf_op jit(solution)/shard_map/ppermute | solution.py:466
  74.5 17.5 %collective-permute-start.14 = (bf16[768,768]{1,0:T(8,128)(2,1)S(1)}, bf16[768,768]{1,0:T(8,128)(2,1)}, u32[]{:S(2)}, u32[]{:S(2)}) collective-permute-start(bf16[768,768]{1,0:T(8,128)(2,1)S(1)} %collective-permute-done.7.refs_3_.refs_4_), channel_id=1, source_target_pairs={{0,8},{8,0},{16,24},{24,16},{32,40},{40,32},{48,56},{56,48},{64,72... | collective-permute-start | bytes 3538952 | tf_op jit(solution)/shard_map/ppermute | solution.py:466
  75.0 17.0 %collective-permute-start.15 = (bf16[768,768]{1,0:T(8,128)(2,1)}, bf16[768,768]{1,0:T(8,128)(2,1)}, u32[]{:S(2)}, u32[]{:S(2)}) collective-permute-start(bf16[768,768]{1,0:T(8,128)(2,1)} %collective-permute-done.8.refs_4_.refs_5_), channel_id=1, source_target_pairs={{0,8},{8,0},{16,24},{24,16},{32,40},{40,32},{48,56},{56,48},{64,72... | collective-permute-start | bytes 3538952 | tf_op jit(solution)/shard_map/ppermute | solution.py:466
  76.2 15.2 %copy-start.11 = (bf16[384,384]{1,0:T(8,128)(2,1)}, bf16[384,384]{1,0:T(8,128)(2,1)S(1)}, u32[]{:S(2)}) copy-start(bf16[384,384]{1,0:T(8,128)(2,1)S(1)} %get-tuple-element.81.refs_0_) | copy-start | bytes 884740
  76.9 9.3 %collective-permute-start.12 = (bf16[384,384]{1,0:T(8,128)(2,1)S(1)}, bf16[384,384]{1,0:T(8,128)(2,1)S(1)}, u32[]{:S(2)}, u32[]{:S(2)}) collective-permute-start(bf16[384,384]{1,0:T(8,128)(2,1)S(1)} %get-tuple-element.62.refs_0_), channel_id=1, source_target_pairs={{0,16},{8,24},{16,0},{24,8},{32,48},{40,56},{48,32},{56,40},{64,80... | collective-permute-start | bytes 884744 | tf_op jit(solution)/shard_map/ppermute | solution.py:471
  77.5 13.9 %collective-permute-start.16 = (bf16[384,768]{1,0:T(8,128)(2,1)}, bf16[384,768]{1,0:T(8,128)(2,1)}, u32[]{:S(2)}, u32[]{:S(2)}) collective-permute-start(bf16[384,768]{1,0:T(8,128)(2,1)} %collective-permute-done.9.refs_7_.refs_8_), channel_id=1, source_target_pairs={{0,8},{8,0},{16,24},{24,16},{32,40},{40,32},{48,56},{56,48},{64,72... | collective-permute-start | bytes 1769480 | tf_op jit(solution)/shard_map/ppermute | solution.py:466
  86.9 5.0 %collective-permute-start.17 = (bf16[384,768]{1,0:T(8,128)(2,1)}, bf16[384,768]{1,0:T(8,128)(2,1)}, u32[]{:S(2)}, u32[]{:S(2)}) collective-permute-start(bf16[384,768]{1,0:T(8,128)(2,1)} %collective-permute-done.10.refs_8_.refs_9_), channel_id=1, source_target_pairs={{0,8},{8,0},{16,24},{24,16},{32,40},{40,32},{48,56},{56,48},{64,72... | collective-permute-start | bytes 1769480 | tf_op jit(solution)/shard_map/ppermute | solution.py:466
  91.4 31.8 %collective-permute-start.11 = (bf16[384,384]{1,0:T(8,128)(2,1)S(1)}, bf16[384,384]{1,0:T(8,128)(2,1)S(1)}, u32[]{:S(2)}, u32[]{:S(2)}) collective-permute-start(bf16[384,384]{1,0:T(8,128)(2,1)S(1)} %get-tuple-element.81.refs_0_), channel_id=1, source_target_pairs={{0,16},{8,24},{16,0},{24,8},{32,48},{40,56},{48,32},{56,40},{64,80... | collective-permute-start | bytes 884744 | tf_op jit(solution)/shard_map/ppermute | solution.py:471
  104.1 14.1 %collective-permute-start.18 = (bf16[384,512]{1,0:T(8,128)(2,1)}, bf16[384,512]{1,0:T(8,128)(2,1)S(1)}, u32[]{:S(2)}, u32[]{:S(2)}) collective-permute-start(bf16[384,512]{1,0:T(8,128)(2,1)} %shard_map.169), channel_id=1, source_target_pairs={{0,16},{8,24},{16,0},{24,8},{32,48},{40,56},{48,32},{56,40},{64,80... | collective-permute-start | bytes 1179656 | tf_op jit(solution)/shard_map/ppermute | solution.py:483
  123.1 29.3 %collective-permute-start.19 = (bf16[384,768]{1,0:T(8,128)(2,1)}, bf16[384,768]{1,0:T(8,128)(2,1)S(1)}, u32[]{:S(2)}, u32[]{:S(2)}) collective-permute-start(bf16[384,768]{1,0:T(8,128)(2,1)} %get-tuple-element.72), channel_id=1, source_target_pairs={{0,2},{1,3},{2,4},{3,5},{4,6},{5,7},{6,0},{7,1},{8,10},{9,11},{10,... | collective-permute-start | bytes 1769480 | tf_op jit(solution)/shard_map/ppermute | solution.py:439
  124.0 28.4 %collective-permute-start.20 = (bf16[384,768]{1,0:T(8,128)(2,1)}, bf16[384,768]{1,0:T(8,128)(2,1)S(1)}, u32[]{:S(2)}, u32[]{:S(2)}) collective-permute-start(bf16[384,768]{1,0:T(8,128)(2,1)} %get-tuple-element.73), channel_id=1, source_target_pairs={{0,4},{1,5},{2,6},{3,7},{4,0},{5,1},{6,2},{7,3},{8,12},{9,13},{10,... | collective-permute-start | bytes 1769480 | tf_op jit(solution)/shard_map/ppermute | solution.py:439
  125.6 27.4 %collective-permute-start.21 = (bf16[384,768]{1,0:T(8,128)(2,1)}, bf16[384,768]{1,0:T(8,128)(2,1)S(1)}, u32[]{:S(2)}, u32[]{:S(2)}) collective-permute-start(bf16[384,768]{1,0:T(8,128)(2,1)} %get-tuple-element.74), channel_id=1, source_target_pairs={{0,6},{1,7},{2,0},{3,1},{4,2},{5,3},{6,4},{7,5},{8,14},{9,15},{10,... | collective-permute-start | bytes 1769480 | tf_op jit(solution)/shard_map/ppermute | solution.py:439
  152.4 14.3 %copy-start.4 = (bf16[384,768]{1,0:T(8,128)(2,1)}, bf16[384,768]{1,0:T(8,128)(2,1)S(1)}, u32[]{:S(2)}) copy-start(bf16[384,768]{1,0:T(8,128)(2,1)S(1)} %collective-permute-done.20.c) | copy-start | bytes 1769476
  153.0 13.7 %collective-permute-start.23 = (bf16[384,512]{1,0:T(8,128)(2,1)}, bf16[384,512]{1,0:T(8,128)(2,1)S(1)}, u32[]{:S(2)}, u32[]{:S(2)}) collective-permute-start(bf16[384,512]{1,0:T(8,128)(2,1)} %shard_map.173), channel_id=1, source_target_pairs={{0,16},{8,24},{16,0},{24,8},{32,48},{40,56},{48,32},{56,40},{64,80... | collective-permute-start | bytes 1179656 | tf_op jit(solution)/shard_map/ppermute | solution.py:483
  172.6 41.7 %all-to-all-start = ((bf16[8,384,384]{2,1,0:T(8,128)(2,1)}), bf16[8,384,384]{2,1,0:T(8,128)(2,1)S(1)}, u32[]{:S(2)}, u32[]{:S(2)}) async-start(bf16[8,384,384]{2,1,0:T(8,128)(2,1)} %shard_map.176), calls=%async_computation | async-start | bytes 4718592 | tf_op jit(solution)/shard_map/all_to_all | solution.py:490
  180.9 33.3 %collective-permute-start.22 = (bf16[384,384]{1,0:T(8,128)(2,1)}, bf16[384,384]{1,0:T(8,128)(2,1)S(1)}, u32[]{:S(2)}, u32[]{:S(2)}) collective-permute-start(bf16[384,384]{1,0:T(8,128)(2,1)} %get-tuple-element.79), channel_id=1, source_target_pairs={{0,1},{1,0},{2,3},{3,2},{4,5},{5,4},{6,7},{7,6},{8,9},{9,8},{10,11... | collective-permute-start | bytes 884744 | tf_op jit(solution)/shard_map/ppermute | solution.py:440
  (17 other events, 90.0 us)
